TPU v7x, 32 devices: a whole 2x2x4 slice. The times are simulated.
32 devices in a mesh: expert: 8 (over y, x, core), tensor: 4 (over z).
Axes of the slice: x: 2, y: 2, z: 4, core: 2. Of those that a mesh axis runs over, the one named last changes fastest.
Arguments:
- tokens: bfloat16 [1024, 7168], P('expert', 'tensor'), may hold values from -6 to 6
- grad_out: bfloat16 [1024, 7168], P('expert', 'tensor'), may hold values from -6 to 6
- expert_ids: int32 [1024, 2], P('expert'), may hold values from 0 to 7, all different within a row; in each aligned block of 128 rows (0 to 127, 128 to 255, ...) at most 64 rows name the same one
- gates: float32 [1024, 2], P('expert'), may hold values from 0.1 to 1
- w_gate: bfloat16 [8, 7168, 2048], P('expert', None, 'tensor'), may hold values from -0.0625 to 0.0625
- w_up: bfloat16 [8, 7168, 2048], P('expert', None, 'tensor'), may hold values from -0.0625 to 0.0625
- w_down: bfloat16 [8, 2048, 7168], P('expert', 'tensor'), may hold values from -0.125 to 0.125
Outputs:
- grad_tokens: bfloat16 [1024, 7168], P('expert', 'tensor')
- grad_w_gate: bfloat16 [8, 7168, 2048], P('expert', None, 'tensor')
- grad_w_up: bfloat16 [8, 7168, 2048], P('expert', None, 'tensor')
- grad_w_down: bfloat16 [8, 2048, 7168], P('expert', 'tensor')
Inputs may be any that keep to these rules, and one draw needn't show every extreme that they name: `expert_ids`: each token names 2 different experts. In each aligned block of 128 tokens (the tokens of one index of the expert axis), no expert is named by more than 64 routes, a bound that some block reaches.
All inputs are finite; a program needn't handle non-finite values.
Results may differ from a plain program's by a relative error of at most 0.0057.
Values may be sent and summed in bfloat16 or wider, within the bound.
No kernel may reach another device: no remote copies, remote signals or barrier semaphores. Data moves between devices by JAX's collectives and lax.ppermute only.
A program may use at most 192 MiB of HBM per device.

v0:
```python
import jax
import jax.numpy as jnp
from jax import lax
from jax.sharding import PartitionSpec as P


def on_device(tokens, grad_out, expert_ids, gates, w_gate, w_up, w_down):
    owners = lax.axis_size("expert")
    tok_rows = tokens.shape[0]
    top_count = expert_ids.shape[1]
    capacity = tok_rows * top_count * 2 // owners
    flat_ids = expert_ids.reshape(-1)
    onehot = (flat_ids[:, None] == jnp.arange(owners, dtype=jnp.int32)[None, :]).astype(jnp.int32)
    before = jnp.cumsum(onehot, axis=0) - onehot
    slot = jnp.sum(before * onehot, axis=1)
    position = flat_ids * capacity + slot
    weighted = (gates[:, :, None] * grad_out[:, None, :].astype(jnp.float32)).astype(jnp.bfloat16)
    weighted = weighted.reshape(tok_rows * top_count, grad_out.shape[1])
    whole_tok, whole_grad = (
        lax.all_gather(tokens, "tensor", axis=1, tiled=True),
        lax.all_gather(weighted, "tensor", axis=1, tiled=True),
    )
    width = whole_tok.shape[1]
    empty = jnp.zeros((owners * capacity, width), jnp.bfloat16)
    send_rows = empty.at[position].set(jnp.repeat(whole_tok, top_count, axis=0))
    send_grads = empty.at[position].set(whole_grad)
    rows_in, grads_in = (
        lax.all_to_all(send_rows, "expert", split_axis=0, concat_axis=0, tiled=True),
        lax.all_to_all(send_grads, "expert", split_axis=0, concat_axis=0, tiled=True),
    )
    wg = w_gate[0]
    wu = w_up[0]
    wd = w_down[0]
    gate = jnp.dot(rows_in, wg, preferred_element_type=jnp.float32)
    upper = jnp.dot(rows_in, wu, preferred_element_type=jnp.float32)
    sig = jax.nn.sigmoid(gate)
    act = gate * sig
    hidden = (act * upper).astype(jnp.bfloat16)
    dhidden = lax.dot_general(
        grads_in, wd, (((1,), (1,)), ((), ())), preferred_element_type=jnp.float32
    )
    dgate = (dhidden * upper * sig * (1.0 + gate * (1.0 - sig))).astype(jnp.bfloat16)
    dup = (dhidden * act).astype(jnp.bfloat16)
    contract_last = (((1,), (1,)), ((), ()))
    partial_dx = lax.dot_general(dgate, wg, contract_last, preferred_element_type=jnp.float32)
    partial_dx = partial_dx + lax.dot_general(
        dup, wu, contract_last, preferred_element_type=jnp.float32
    )
    contract_first = (((0,), (0,)), ((), ()))
    grad_wg = lax.dot_general(
        rows_in, dgate, contract_first, preferred_element_type=jnp.float32
    ).astype(jnp.bfloat16)
    grad_wu = lax.dot_general(
        rows_in, dup, contract_first, preferred_element_type=jnp.float32
    ).astype(jnp.bfloat16)
    grad_wd = lax.dot_general(
        hidden, grads_in, contract_first, preferred_element_type=jnp.float32
    ).astype(jnp.bfloat16)
    shares = lax.psum_scatter(partial_dx, "tensor", scatter_dimension=1, tiled=True)
    returned = lax.all_to_all(shares, "expert", split_axis=0, concat_axis=0, tiled=True)
    picked = returned[position]
    grad_tokens = jnp.sum(picked.reshape(tok_rows, top_count, picked.shape[1]), axis=1).astype(
        jnp.bfloat16
    )
    return (grad_tokens, grad_wg[None], grad_wu[None], grad_wd[None])


def solution(mesh):
    placed = (
        P("expert", "tensor"),
        P("expert", "tensor"),
        P("expert", None),
        P("expert", None),
        P("expert", None, "tensor"),
        P("expert", None, "tensor"),
        P("expert", "tensor", None),
    )
    return jax.shard_map(
        on_device,
        mesh=mesh,
        in_specs=placed,
        out_specs=(
            P("expert", "tensor"),
            P("expert", None, "tensor"),
            P("expert", None, "tensor"),
            P("expert", "tensor", None),
        ),
        check_vma=False,
    )
```

profile of v0, /device:TPU:0, one launch (start us, length us, event | category | flops | bytes accessed | tf_op | source)
XLA Modules:
  0.0 601.6 jit_solution(14395015208366500930)
XLA Ops:
  10.9 42.8 %all-gather.5.cloned.1.call-done = bf16[128,7168]{1,0:T(8,128)(2,1)} async-done(((bf16[128,1792]{1,0:T(8,128)(2,1)}), bf16[128,7168]{1,0:T(8,128)(2,1)}) %all-gather.5.cloned.1.call-update) | async-done | bytes 1835024 | tf_op jit(solution)/shard_map/all_gather | solution.py:20
  53.7 4.9 broadcast_in_dim.22
  58.6 8.4 %reshape.96 = bf16[256,7168]{1,0:T(8,128)(2,1)} reshape(bf16[128,2,7168]{2,1,0:T(2,128)(2,1)} %broadcast_in_dim.22) | data formatting | bytes 7340032 | tf_op jit(solution)/shard_map/reshape | solution.py:25
  67.0 11.1 %scatter_custom_fusion.1 = bf16[512,7168]{1,0:T(8,128)(2,1)} fusion(s32[256]{0:T(256)S(1)} %bitcast.52, bf16[256,7168]{1,0:T(8,128)(2,1)} %reshape.96, bf16[]{:T(256)} %constant.6.clone.1), kind=kCustom, calls=%fused_computation.19 | custom fusion | bytes 7340544 | tf_op jit(solution)/shard_map/scatter | solution.py:25
  78.1 5.0 all-to-all-start.1
  85.1 2.5 mul.65
  89.0 71.7 %all-gather.3.cloned.1.call-done = bf16[256,7168]{1,0:T(8,128)(2,1)} async-done(((bf16[256,1792]{1,0:T(8,128)(2,1)}), bf16[256,7168]{1,0:T(8,128)(2,1)}) %all-gather.3.cloned.1.call-update) | async-done | bytes 3670032 | tf_op jit(solution)/shard_map/all_gather | solution.py:21
  160.7 11.1 %scatter_custom_fusion = bf16[512,7168]{1,0:T(8,128)(2,1)} fusion(s32[256]{0:T(256)S(1)} %bitcast.53, bf16[256,7168]{1,0:T(8,128)(2,1)} %all-gather.3.cloned.1.call-done, bf16[]{:T(256)} %constant.6.clone.1), kind=kCustom, calls=%fused_computation.21 | custom fusion | bytes 7340544 | tf_op jit(solution)/shard_map/scatter | solution.py:26
  171.8 5.1 all-to-all-start
  177.2 10.2 %fusion.5 = f32[512,512]{1,0:T(8,128)} fusion(bf16[512,7168]{1,0:T(8,128)(2,1)} %bitcast.8, bf16[1,7168,512]{2,1,0:T(8,128)(2,1)} %param.11), kind=kOutput, calls=%fused_computation.12 | convolution fusion | flops 3758096384 | bytes 15728640 | tf_op jit(solution)/shard_map/dot_general | solution.py:34
  187.5 7.1 %fusion.8 = f32[512,512]{1,0:T(8,128)} fusion(bf16[512,7168]{1,0:T(8,128)(2,1)} %bitcast.8, bf16[1,7168,512]{2,1,0:T(8,128)(2,1)S(1)} %bitcast.50), kind=kOutput, calls=%fused_computation.15 | convolution fusion | flops 3758096384 | bytes 15728640 | tf_op jit(solution)/shard_map/dot_general | solution.py:35
  194.6 65.2 %all-to-all-done = bf16[8,64,7168]{2,1,0:T(8,128)(2,1)} async-done(((bf16[8,64,7168]{2,1,0:T(8,128)(2,1)}), bf16[8,64,7168]{2,1,0:T(8,128)(2,1)}, u32[]{:S(2)}, u32[]{:S(2)}) %all-to-all-start) | async-done | bytes 7340064 | tf_op jit(solution)/shard_map/all_to_all | solution.py:29
  259.8 9.9 %multiply_convert_fusion.2 = (bf16[512,512]{1,0:T(8,128)(2,1)S(1)}, bf16[512,512]{1,0:T(8,128)(2,1)S(1)}) fusion(f32[512,512]{1,0:T(8,128)} %fusion.5, f32[512,512]{1,0:T(8,128)} %fusion.8, bf16[512,7168]{1,0:T(8,128)(2,1)} %bitcast.5, bf16[1,512,7168]{2,1,0:T(8,128)(2,1)} %param.13), kind=kOutput, calls=%fused_computation.25 | convolution fusion | flops 3761504256 | bytes 17825792 | tf_op jit(solution)/shard_map/dot_general | solution.py:39
  269.7 10.4 %fusion.3 = f32[512,7168]{1,0:T(8,128)} fusion(bf16[512,512]{1,0:T(8,128)(2,1)S(1)} %get-tuple-element.5, bf16[1,7168,512]{2,1,0:T(8,128)(2,1)} %param.11), kind=kOutput, calls=%fused_computation.10 | convolution fusion | flops 3758096384 | bytes 22544384 | tf_op jit(solution)/shard_map/dot_general | solution.py:45
  280.1 12.5 %convolution_add_fusion = f32[512,7168]{1,0:T(8,128)} fusion(f32[512,7168]{1,0:T(8,128)} %fusion.3, bf16[512,512]{1,0:T(8,128)(2,1)S(1)} %get-tuple-element.4, bf16[1,7168,512]{2,1,0:T(8,128)(2,1)} %param.12), kind=kOutput, calls=%fused_computation.3 | convolution fusion | flops 3761766400 | bytes 37224448 | tf_op jit(solution)/shard_map/dot_general | solution.py:46
  292.7 242.7 %reduce-scatter.2.cloned.1.call-done = f32[512,1792]{1,0:T(8,128)} async-done(((f32[512,7168]{1,0:T(8,128)}), f32[512,1792]{1,0:T(8,128)}) %reduce-scatter.2.cloned.1.call-update) | async-done | bytes 3670032 | tf_op jit(solution)/shard_map/reduce_scatter | solution.py:59
  535.3 4.8 all-to-all-start.2
  540.1 9.3 %fusion.2 = bf16[1,512,7168]{2,1,0:T(8,128)(2,1)} fusion(bf16[512,7168]{1,0:T(8,128)(2,1)} %bitcast.5, f32[512,512]{1,0:T(8,128)S(1)} %copy-done.1, f32[512,512]{1,0:T(8,128)S(1)} %copy-done), kind=kOutput, calls=%fused_computation.9 | convolution fusion | flops 3763339264 | bytes 16777216 | tf_op jit(solution)/shard_map/dot_general | solution.py:56
  549.4 9.2 %fusion = bf16[1,7168,512]{2,1,0:T(8,128)(2,1)} fusion(bf16[512,7168]{1,0:T(8,128)(2,1)} %bitcast.8, bf16[512,512]{1,0:T(8,128)(2,1)S(1)} %get-tuple-element.5), kind=kOutput, calls=%fused_computation.7 | convolution fusion | flops 3761766400 | bytes 15204352 | tf_op jit(solution)/shard_map/dot_general | solution.py:50
  558.6 9.2 %fusion.1 = bf16[1,7168,512]{2,1,0:T(8,128)(2,1)} fusion(bf16[512,7168]{1,0:T(8,128)(2,1)} %bitcast.8, bf16[512,512]{1,0:T(8,128)(2,1)S(1)} %get-tuple-element.4), kind=kOutput, calls=%fused_computation.8 | convolution fusion | flops 3761766400 | bytes 15204352 | tf_op jit(solution)/shard_map/dot_general | solution.py:53
  567.8 15.8 %all-to-all-done.2 = f32[8,64,1792]{2,1,0:T(8,128)} async-done(((f32[8,64,1792]{2,1,0:T(8,128)}), f32[8,64,1792]{2,1,0:T(8,128)}, u32[]{:S(2)}, u32[]{:S(2)}) %all-to-all-start.2) | async-done | bytes 3670048 | tf_op jit(solution)/shard_map/all_to_all | solution.py:60
  583.6 4.2 gather_fusion
  587.8 2.3 reshape.75
  590.2 4.5 reduce_sum.22
  (38 shorter events, 7.3 us)
Async XLA Ops:
  7.2 46.5 %all-gather.5.cloned.1.call-start = ((), (), s32[]{:S(2)}) async-start(), calls=%async_computation.5 | async-start | bytes 2293760 | tf_op jit(solution)/shard_map/all_gather | solution.py:20
  78.1 5.2 copy-start.2
  78.1 9.5 %copy-start.3 = (f32[128,2]{0,1:T(2,128)S(1)}, f32[128,2]{0,1:T(2,128)}, u32[]{:S(2)}) copy-start(f32[128,2]{0,1:T(2,128)} %param.10) | copy-start | bytes 3076
  78.1 93.7 %all-to-all-start.1 = ((bf16[8,64,7168]{2,1,0:T(8,128)(2,1)}), bf16[8,64,7168]{2,1,0:T(8,128)(2,1)}, u32[]{:S(2)}, u32[]{:S(2)}) async-start(bf16[8,64,7168]{2,1,0:T(8,128)(2,1)} %bitcast.47), calls=%async_computation.1 | async-start | bytes 14680064 | tf_op jit(solution)/shard_map/all_to_all | solution.py:28
  83.1 77.5 %all-gather.3.cloned.1.call-start = ((), (), s32[]{:S(2)}) async-start(), calls=%async_computation.4 | async-start | bytes 4587520 | tf_op jit(solution)/shard_map/all_gather | solution.py:21
  171.8 15.7 %slice-start = ((s8[7340032]{0:T(1024)(128)(4,1)}), s8[3145728]{0:T(1024)(128)(4,1)S(1)}, s32[]{:S(2)}) async-start(s8[7340032]{0:T(1024)(128)(4,1)} %bitcast.49), calls=%async_computation.7 | async-start | bytes 6291456
  171.8 88.0 %all-to-all-start = ((bf16[8,64,7168]{2,1,0:T(8,128)(2,1)}), bf16[8,64,7168]{2,1,0:T(8,128)(2,1)}, u32[]{:S(2)}, u32[]{:S(2)}) async-start(bf16[8,64,7168]{2,1,0:T(8,128)(2,1)} %bitcast.48), calls=%async_computation | async-start | bytes 14680064 | tf_op jit(solution)/shard_map/all_to_all | solution.py:29
  176.9 358.4 %reduce-scatter.2.cloned.1.call-start = ((), (), s32[]{:S(2)}) async-start(), calls=%async_computation.6 | async-start | bytes 18350080 | tf_op jit(solution)/shard_map/reduce_scatter | solution.py:59
  177.2 10.3 %slice-start.1 = ((s8[7340032]{0:T(1024)(128)(4,1)}), s8[4194304]{0:T(1024)(128)(4,1)S(1)}, s32[]{:S(2)}) async-start(s8[7340032]{0:T(1024)(128)(4,1)} %bitcast.49), calls=%async_computation.8 | async-start | bytes 8388608
  292.7 247.5 %copy-start = (f32[512,512]{1,0:T(8,128)S(1)}, f32[512,512]{1,0:T(8,128)}, u32[]{:S(2)}) copy-start(f32[512,512]{1,0:T(8,128)} %fusion.5) | copy-start | bytes 3145732
  292.7 247.5 %copy-start.1 = (f32[512,512]{1,0:T(8,128)S(1)}, f32[512,512]{1,0:T(8,128)}, u32[]{:S(2)}) copy-start(f32[512,512]{1,0:T(8,128)} %fusion.8) | copy-start | bytes 3145732
  535.3 48.3 %all-to-all-start.2 = ((f32[8,64,1792]{2,1,0:T(8,128)}), f32[8,64,1792]{2,1,0:T(8,128)}, u32[]{:S(2)}, u32[]{:S(2)}) async-start(f32[8,64,1792]{2,1,0:T(8,128)} %bitcast.51), calls=%async_computation.3 | async-start | bytes 7340032 | tf_op jit(solution)/shard_map/all_to_all | solution.py:60
Sparse Core Ops, SparseCore 0:
  9.6 44.0 all-gather.4
  89.1 71.5 all-gather.2
  292.8 242.5 reduce-scatter.1
where the time goes:
time: 610 us; the launch traced here: 602 us
  waiting for transfers between devices  439 us (72%)
  matrix products  77.9 us (13%)
  local copies, waits for them, and re-layouts  48.2 us (8%)
  starting transfers between devices  15.4 us (3%)
  between operations  14.3 us (2%)
  other arithmetic  7.01 us (1%)
    reduce_scatter x1, waiting for transfers between devices, on_device(): lax.psum_scatter(partial_dx, 'tensor', scatter_dimension=1, tiled=True)  243 us
    all_gather x1, waiting for transfers between devices, on_device(): lax.all_gather(weighted, 'tensor', axis=1, tiled=True)  71.7 us
    all_to_all x1, waiting for transfers between devices, on_device(): lax.all_to_all(send_grads, 'expert', split_axis=0, concat_axis=0, tiled=T...  65.2 us
    all_gather x1, waiting for transfers between devices, on_device(): lax.all_gather(tokens, 'tensor', axis=1, tiled=True)  42.8 us
    all_to_all x1, waiting for transfers between devices, on_device(): lax.all_to_all(shares, 'expert', split_axis=0, concat_axis=0, tiled=True)  15.8 us
    dot_general x1, matrix products, on_device(): lax.dot_general(dup, wu, contract_last, preferred_element_type=jnp.float32)  12.5 us
  transfers between devices with their start and end apart: 6, of which 5 were waited for; matrix products, arithmetic and copies ran while one was open for 11% of the time, Pallas kernels for 0%

commit v1 on v0

v1 whole, which is shorter than its diff:
```python
import functools

import jax
import jax.numpy as jnp
from jax import lax
from jax.sharding import PartitionSpec as P

BF16 = jnp.bfloat16
F32 = jnp.float32


def swap(a, mask):
    n = lax.axis_size("expert")
    return lax.ppermute(a, "expert", [(i, i ^ mask) for i in range(n)])


def ring(a):
    n = lax.axis_size("tensor")
    return lax.ppermute(a, "tensor", [(i, (i + 1) % n) for i in range(n)])


def far_masks():
    n = lax.axis_size("expert")
    return [1 << b for b in range(1, n.bit_length() - 1)]


def block_order():
    n = lax.axis_size("expert")
    near = [0]
    for m in far_masks():
        near = near + [k ^ m for k in near]
    return near + [k ^ 1 for k in near]


def gather_rows(own):
    far = far_masks()
    if len(far) == 2:
        h = own.shape[0] // 2
        x = swap(own, far[0])
        y = swap(own, far[1])
        da = swap(x[:h], far[1])
        db = swap(y[h:], far[0])
        pieces = [own, x, y, da, db]
    else:
        pieces = [own]
        for m in far:
            pieces = pieces + [swap(p, m) for p in pieces]
    return pieces + [swap(p, 1) for p in pieces]


def scatter_rows(part, rows):
    half = part.shape[0] // 2
    far = far_masks()
    got = swap(part[half:], 1)
    mine = part[:half].astype(F32) + got.astype(F32)
    mine = mine.astype(BF16).reshape(half // rows, rows, -1)
    if len(far) == 2:
        h = rows // 2
        ex = swap(mine[3, :h], far[0])
        ey = swap(mine[3, h:], far[1])
        fx_a = swap(mine[1, :h], far[0])
        fy_b = swap(mine[2, h:], far[1])
        fy_a = swap((mine[2, :h].astype(F32) + ex.astype(F32)).astype(BF16), far[1])
        fx_b = swap((mine[1, h:].astype(F32) + ey.astype(F32)).astype(BF16), far[0])
        return [
            mine[0],
            jnp.concatenate([fx_a, fx_b]),
            jnp.concatenate([fy_a, fy_b]),
        ]
    for m in reversed(far):
        cut = mine.shape[0] // 2
        got = swap(mine[cut:], m)
        mine = (mine[:cut].astype(F32) + got.astype(F32)).astype(BF16)
    return [mine[0]]


def total(terms):
    return functools.reduce(lambda a, b: a + b, [t.astype(F32) for t in terms])


def on_device(tokens, grad_out, expert_ids, gates, w_gate, w_up, w_down):
    owners, shards = lax.axis_size("expert"), lax.axis_size("tensor")
    me, z = lax.axis_index("expert"), lax.axis_index("tensor")
    rows, width = tokens.shape
    wg, wu, wd = w_gate[0], w_up[0], w_down[0]
    order = block_order()

    chosen = expert_ids[:, :, None] == jnp.arange(owners, dtype=jnp.int32)
    weights = jnp.sum(jnp.where(chosen, gates[:, :, None], 0.0), axis=1)
    weights = lax.all_to_all(weights.T, "expert", split_axis=0, concat_axis=0, tiled=True)
    weights = weights[me ^ jnp.array(order, dtype=jnp.int32)].reshape(-1, 1)

    at = [lax.rem(z - j + shards, shards) * width for j in range(shards)]
    cut_rows = lambda w, j: lax.dynamic_slice_in_dim(w, at[j], width, 0)
    cut_cols = lambda w, j: lax.dynamic_slice_in_dim(w, at[j], width, 1)

    def gather(own):
        out = []
        for j in range(shards):
            if j:
                own = ring(own)
            out.append(gather_rows(own))
        return out

    x = [jnp.concatenate(p) for p in gather(tokens)]
    gate = total([jnp.dot(x[j], cut_rows(wg, j), preferred_element_type=F32) for j in range(shards)])
    upper = total([jnp.dot(x[j], cut_rows(wu, j), preferred_element_type=F32) for j in range(shards)])
    g = [(weights * jnp.concatenate(p).astype(F32)).astype(BF16) for p in gather(grad_out)]
    last = (((1,), (1,)), ((), ()))
    first = (((0,), (0,)), ((), ()))
    dot = functools.partial(lax.dot_general, preferred_element_type=F32)
    dhidden = total([dot(g[j], cut_cols(wd, j), last) for j in range(shards)])

    sig = jax.nn.sigmoid(gate)
    act = gate * sig
    hidden = (act * upper).astype(BF16)
    dgate = (dhidden * upper * sig * (1.0 + gate * (1.0 - sig))).astype(BF16)
    dup = (dhidden * act).astype(BF16)

    run = None
    for j in list(range(1, shards)) + [0]:
        part = dot(dgate, cut_rows(wg, j), last) + dot(dup, cut_rows(wu, j), last)
        terms = scatter_rows(part.astype(BF16), rows)
        if run is not None:
            terms.append(ring(run))
        run = total(terms).astype(BF16)

    grad_wg = jnp.zeros(wg.shape, BF16)
    grad_wu = jnp.zeros(wu.shape, BF16)
    grad_wd = jnp.zeros(wd.shape, BF16)
    for j in range(shards):
        grad_wg = lax.dynamic_update_slice_in_dim(grad_wg, dot(x[j], dgate, first).astype(BF16), at[j], 0)
        grad_wu = lax.dynamic_update_slice_in_dim(grad_wu, dot(x[j], dup, first).astype(BF16), at[j], 0)
        grad_wd = lax.dynamic_update_slice_in_dim(grad_wd, dot(hidden, g[j], first).astype(BF16), at[j], 1)
    return (run, grad_wg[None], grad_wu[None], grad_wd[None])


def solution(mesh):
    placed = (
        P("expert", "tensor"),
        P("expert", "tensor"),
        P("expert", None),
        P("expert", None),
        P("expert", None, "tensor"),
        P("expert", None, "tensor"),
        P("expert", "tensor", None),
    )
    return jax.shard_map(
        on_device,
        mesh=mesh,
        in_specs=placed,
        out_specs=(
            P("expert", "tensor"),
            P("expert", None, "tensor"),
            P("expert", None, "tensor"),
            P("expert", "tensor", None),
        ),
        check_vma=False,
    )
```

time: 610 us -> 391 us (0.64)
  waiting for transfers between devices: 439 us -> 130 us
  starting transfers between devices: 15.4 us -> 80 us
  matrix products: 77.9 us -> 139 us
  local copies, waits for them, and re-layouts: 48.2 us -> 20.5 us
  between operations: 14.3 us -> 2.46 us
    reduce_scatter x1 -> x0, waiting for transfers between devices: 243 us -> none  [on_device(): lax.psum_scatter(partial_dx, 'tensor', scatter_dimension=1, tiled=True)]
    ppermute x0 -> x109, waiting for transfers between devices: none -> 130 us  [the longest x100 107 us: swap(): return lax.ppermute(a, 'expert', [(i, i ^ mask) for i in range(n)])]
    all_gather x2 -> x0, waiting for transfers between devices: 115 us -> none  [the longest x1 71.7 us: on_device(): lax.all_gather(weighted, 'tensor', axis=1, tiled=True)]
    all_to_all x3 -> x1, waiting for transfers between devices: 81 us -> 0.47 us  [on_device(): lax.all_to_all(weights.T, 'expert', split_axis=0, concat_axis=0, tiled=True)]
    ppermute x0 -> x109, starting transfers between devices: none -> 76.7 us  [the longest x100 69.4 us: swap(): return lax.ppermute(a, 'expert', [(i, i ^ mask) for i in range(n)])]
    dot_general x8 -> x32, matrix products: 77.9 us -> 139 us  [the longest x8 45.3 us: on_device(): part = dot(dgate, cut_rows(wg, j), last) + dot(dup, cut_rows(wu, j), last)]
    scatter x2 -> x0, local copies, waits for them, and re-layouts: 22.3 us -> none  [the longest x1 11.1 us: on_device(): send_rows = empty.at[position].set(jnp.repeat(whole_tok, top_count, axis=0))]
    unnamed x14 -> x126, local copies, waits for them, and re-layouts: 0.93 us -> 13.3 us
  transfers between devices with their start and end apart: 6 -> 110, of which waited for: 5 -> 45; matrix products, arithmetic and copies ran while one was open for 11% -> 25% of each run, Pallas kernels for 0% -> 0%
where the time goes in v1:
time: 391 us; the launch traced here: 384 us
  matrix products  139 us (36%)
  waiting for transfers between devices  130 us (33%)
  starting transfers between devices  80 us (20%)
  local copies, waits for them, and re-layouts  20.5 us (5%)
  other arithmetic  11.8 us (3%)
    ppermute x100, waiting for transfers between devices, swap(): return lax.ppermute(a, 'expert', [(i, i ^ mask) for i in range(n)])  107 us
    ppermute x100, starting transfers between devices, swap(): return lax.ppermute(a, 'expert', [(i, i ^ mask) for i in range(n)])  69.4 us
    dot_general x8, matrix products, on_device(): part = dot(dgate, cut_rows(wg, j), last) + dot(dup, cut_rows(wu, j), last)  45.3 us
    dot_general x4, matrix products, on_device(): dhidden = total([dot(g[j], cut_cols(wd, j), last) for j in range(shards)])  23.7 us
    ppermute x9, waiting for transfers between devices, ring(): return lax.ppermute(a, 'tensor', [(i, (i + 1) % n) for i in range(n)])  23.2 us
    dot_general x4, matrix products, on_device(): jnp.dot(x[j], cut_rows(wu, j), preferred_element_type=F32)  22.1 us
    dot_general x4, matrix products, on_device(): jnp.dot(x[j], cut_rows(wg, j), preferred_element_type=F32)  15.3 us
    unnamed x126, local copies, waits for them, and re-layouts  13.3 us
  transfers between devices with their start and end apart: 110, of which 45 were waited for; matrix products, arithmetic and copies ran while one was open for 25% of the time, Pallas kernels for 0%

profile of v1, /device:TPU:0, one launch (start us, length us, event | category | flops | bytes accessed | tf_op | source)
XLA Modules:
  0.0 383.9 jit_solution(12961429436351827330)
XLA Ops:
  48.0 6.8 %collective-permute-done.10 = bf16[128,1792]{1,0:T(8,128)(2,1)S(1)} collective-permute-done((bf16[128,1792]{1,0:T(8,128)(2,1)S(1)}, bf16[128,1792]{1,0:T(8,128)(2,1)S(1)}, u32[]{:S(2)}, u32[]{:S(2)}) %collective-permute-start.10) | collective-permute-done | bytes 458784 | tf_op jit(solution)/shard_map/ppermute | solution.py:14
  61.1 8.4 %collective-permute-done.58 = bf16[128,1792]{1,0:T(8,128)(2,1)S(1)} collective-permute-done((bf16[128,1792]{1,0:T(8,128)(2,1)S(1)}, bf16[128,1792]{1,0:T(8,128)(2,1)S(1)}, u32[]{:S(2)}, u32[]{:S(2)}) %collective-permute-start.58) | collective-permute-done | bytes 458784 | tf_op jit(solution)/shard_map/ppermute | solution.py:19
  70.3 5.2 %fusion.59 = f32[1024,512]{1,0:T(8,128)} fusion(bf16[1,512,7168]{2,1,0:T(8,128)(2,1)} %param.14, s32[]{:T(128)S(6)} %select_n.16, bf16[1024,1792]{1,0:T(8,128)(2,1)S(1)} %constant_dynamic-update-slice_fusion, f32[1024]{0:T(1024)S(1)} %bitcast.236), kind=kOutput, calls=%fused_computation.91 | convolution fusion | flops 1884553216 | bytes 7606276 | tf_op jit(solution)/shard_map/dot_general | solution.py:112
  82.6 4.9 %fusion.51 = f32[1024,512]{1,0:T(8,128)} fusion(bf16[1024,1792]{1,0:T(8,128)(2,1)S(1)} %constant_dynamic-update-slice_fusion.40, bf16[1,7168,512]{2,1,0:T(8,128)(2,1)} %param.13, s32[]{:T(128)S(6)} %select_n.16), kind=kOutput, calls=%fused_computation.83 | convolution fusion | flops 1879048192 | bytes 7602180 | tf_op jit(solution)/shard_map/dot_general | solution.py:107
  98.4 8.5 %collective-permute-done.20 = bf16[128,1792]{1,0:T(8,128)(2,1)S(1)} collective-permute-done((bf16[128,1792]{1,0:T(8,128)(2,1)S(1)}, bf16[128,1792]{1,0:T(8,128)(2,1)S(1)}, u32[]{:S(2)}, u32[]{:S(2)}) %collective-permute-start.20) | collective-permute-done | bytes 458784 | tf_op jit(solution)/shard_map/ppermute | solution.py:14
  107.0 8.0 %collective-permute-done.59 = bf16[128,1792]{1,0:T(8,128)(2,1)S(1)} collective-permute-done((bf16[128,1792]{1,0:T(8,128)(2,1)S(1)}, bf16[128,1792]{1,0:T(8,128)(2,1)S(1)}, u32[]{:S(2)}, u32[]{:S(2)}) %collective-permute-start.59) | collective-permute-done | bytes 458784 | tf_op jit(solution)/shard_map/ppermute | solution.py:14
  116.1 5.5 %collective-permute-done.29 = bf16[128,1792]{1,0:T(8,128)(2,1)S(1)} collective-permute-done((bf16[128,1792]{1,0:T(8,128)(2,1)S(1)}, bf16[128,1792]{1,0:T(8,128)(2,1)S(1)}, u32[]{:S(2)}, u32[]{:S(2)}) %collective-permute-start.29) | collective-permute-done | bytes 458784 | tf_op jit(solution)/shard_map/ppermute | solution.py:19
  126.5 5.0 %fusion.57 = f32[1024,512]{1,0:T(8,128)} fusion(bf16[1,512,7168]{2,1,0:T(8,128)(2,1)} %param.14, s32[]{:T(128)S(6)} %select_n.17, bf16[1024,1792]{1,0:T(8,128)(2,1)S(1)} %constant_dynamic-update-slice_fusion.10, f32[1024]{0:T(1024)S(1)} %bitcast.237), kind=kOutput, calls=%fused_computation.89 | convolution fusion | flops 1884553216 | bytes 7606276 | tf_op jit(solution)/shard_map/dot_general | solution.py:112
  140.2 4.9 %fusion.48 = f32[1024,512]{1,0:T(8,128)} fusion(bf16[1024,1792]{1,0:T(8,128)(2,1)S(1)} %constant_dynamic-update-slice_fusion.50, bf16[1,7168,512]{2,1,0:T(8,128)(2,1)} %param.13, s32[]{:T(128)S(6)} %select_n.17), kind=kOutput, calls=%fused_computation.80 | convolution fusion | flops 1879048192 | bytes 7602180 | tf_op jit(solution)/shard_map/dot_general | solution.py:107
  154.5 9.3 %collective-permute-done.30 = bf16[128,1792]{1,0:T(8,128)(2,1)S(1)} collective-permute-done((bf16[128,1792]{1,0:T(8,128)(2,1)S(1)}, bf16[128,1792]{1,0:T(8,128)(2,1)S(1)}, u32[]{:S(2)}, u32[]{:S(2)}) %collective-permute-start.30) | collective-permute-done | bytes 458784 | tf_op jit(solution)/shard_map/ppermute | solution.py:14
  170.0 4.9 %fusion.55 = f32[1024,512]{1,0:T(8,128)} fusion(bf16[1,512,7168]{2,1,0:T(8,128)(2,1)} %param.14, s32[]{:T(128)S(6)} %select_n.18, bf16[1024,1792]{1,0:T(8,128)(2,1)S(1)} %constant_dynamic-update-slice_fusion.20, f32[1024]{0:T(1024)S(1)} %bitcast.238), kind=kOutput, calls=%fused_computation.87 | convolution fusion | flops 1884553216 | bytes 7606276 | tf_op jit(solution)/shard_map/dot_general | solution.py:112
  179.1 4.9 %fusion.31 = f32[1024,512]{1,0:T(8,128)S(1)} fusion(bf16[1024,1792]{1,0:T(8,128)(2,1)S(1)} %constant_dynamic-update-slice_fusion.60, bf16[1,7168,512]{2,1,0:T(8,128)(2,1)} %param.12, s32[]{:T(128)S(6)} %select_n.18), kind=kOutput, calls=%fused_computation.63 | convolution fusion | flops 1879048192 | bytes 7602180 | tf_op jit(solution)/shard_map/dot_general | solution.py:106
  185.0 4.9 %fusion.45 = f32[1024,512]{1,0:T(8,128)} fusion(bf16[1024,1792]{1,0:T(8,128)(2,1)S(1)} %constant_dynamic-update-slice_fusion.60, bf16[1,7168,512]{2,1,0:T(8,128)(2,1)} %param.13, s32[]{:T(128)S(6)} %select_n.18), kind=kOutput, calls=%fused_computation.77 | convolution fusion | flops 1879048192 | bytes 7602180 | tf_op jit(solution)/shard_map/dot_general | solution.py:107
  200.6 8.6 %add_add_fusion.2 = f32[1024,512]{1,0:T(8,128)} fusion(f32[1024,512]{1,0:T(8,128)} %fusion.55, f32[1024,512]{1,0:T(8,128)} %fusion.59, f32[1024,512]{1,0:T(8,128)} %fusion.57, bf16[1,512,7168]{2,1,0:T(8,128)(2,1)} %param.14, s32[]{:T(128)S(6)} %select_n.19, bf16[1024,1792]{1,0:T(8,128)(2,1)S(1)} %constant_dynamic-update-slice_fusion.30, f32[1024]{0:T(1024)S(1)} %bitcast.239), kind=kOutput, calls=%fused_computation.56 | convolution fusion | flops 1886126080 | bytes 13897732 | tf_op jit(solution)/shard_map/dot_general | solution.py:112
  209.3 5.0 %add_add_fusion = f32[1024,512]{1,0:T(8,128)S(1)} fusion(f32[1024,512]{1,0:T(8,128)S(1)} %fusion.31, f32[1024,512]{1,0:T(8,128)S(1)} %fusion.39, f32[1024,512]{1,0:T(8,128)S(1)} %copy-done.17, bf16[1024,1792]{1,0:T(8,128)(2,1)S(1)} %constant_dynamic-update-slice_fusion.70, bf16[1,7168,512]{2,1,0:T(8,128)(2,1)} %param.12, s32[]{:T(128)S(6)} %select_n.19), kind=kOutput, calls=%fused_computation.54 | convolution fusion | flops 1880621056 | bytes 13893636 | tf_op jit(solution)/shard_map/dot_general | solution.py:106
  214.3 7.4 %multiply_convert_fusion.4 = (bf16[1024,512]{1,0:T(8,128)(2,1)S(1)}, bf16[1024,512]{1,0:T(8,128)(2,1)S(1)}, bf16[1024,512]{1,0:T(8,128)(2,1)}) fusion(f32[1024,512]{1,0:T(8,128)S(1)} %add_add_fusion, f32[1024,512]{1,0:T(8,128)S(1)} %copy-done.20, bf16[1024,1792]{1,0:T(8,128)(2,1)S(1)} %constant_dynamic-update-slice_fusion.70, ...), kind=kOutput, calls=%fused_computation.49 | convolution fusion | flops 1888485376 | bytes 19136516 | tf_op jit(solution)/shard_map/dot_general | solution.py:107
  221.8 7.0 %fusion.37 = f32[1024,1792]{1,0:T(8,128)} fusion(bf16[1024,512]{1,0:T(8,128)(2,1)S(1)} %get-tuple-element.5, bf16[1,7168,512]{2,1,0:T(8,128)(2,1)} %param.12, s32[]{:T(128)S(6)} %select_n.16), kind=kOutput, calls=%fused_computation.69 | convolution fusion | flops 1879048192 | bytes 10223620 | tf_op jit(solution)/shard_map/dot_general | solution.py:122
  228.7 6.8 %fusion.25 = f32[1024,1792]{1,0:T(8,128)} fusion(bf16[1024,512]{1,0:T(8,128)(2,1)S(1)} %get-tuple-element.5, bf16[1,7168,512]{2,1,0:T(8,128)(2,1)} %param.12, s32[]{:T(128)S(6)} %select_n.19), kind=kOutput, calls=%fused_computation.57 | convolution fusion | flops 1879048192 | bytes 10223620 | tf_op jit(solution)/shard_map/dot_general | solution.py:122
  235.5 5.2 %fusion.29 = f32[1024,1792]{1,0:T(8,128)} fusion(bf16[1024,512]{1,0:T(8,128)(2,1)S(1)} %get-tuple-element.5, bf16[1,7168,512]{2,1,0:T(8,128)(2,1)S(1)} %bitcast.247, s32[]{:T(128)S(6)} %select_n.18), kind=kOutput, calls=%fused_computation.61 | convolution fusion | flops 1879048192 | bytes 10223620 | tf_op jit(solution)/shard_map/dot_general | solution.py:122
  240.7 5.2 %fusion.33 = f32[1024,1792]{1,0:T(8,128)} fusion(bf16[1024,512]{1,0:T(8,128)(2,1)S(1)} %get-tuple-element.5, bf16[1,7168,512]{2,1,0:T(8,128)(2,1)S(1)} %bitcast.247, s32[]{:T(128)S(6)} %select_n.17), kind=kOutput, calls=%fused_computation.65 | convolution fusion | flops 1879048192 | bytes 10223620 | tf_op jit(solution)/shard_map/dot_general | solution.py:122
  275.4 5.9 %add_convert_fusion.3 = bf16[1024,1792]{1,0:T(8,128)(2,1)S(1)} fusion(f32[1024,1792]{1,0:T(8,128)} %fusion.37, bf16[1024,512]{1,0:T(8,128)(2,1)S(1)} %copy-done.16, bf16[1,7168,512]{2,1,0:T(8,128)(2,1)} %param.13, s32[]{:T(128)S(6)} %select_n.16), kind=kOutput, calls=%fused_computation.4 | convolution fusion | flops 1882718208 | bytes 13893636 | tf_op jit(solution)/shard_map/dot_general | solution.py:122
  288.2 5.9 %add_convert_fusion = bf16[1024,1792]{1,0:T(8,128)(2,1)S(1)} fusion(f32[1024,1792]{1,0:T(8,128)} %fusion.33, bf16[1024,512]{1,0:T(8,128)(2,1)S(1)} %copy-done.16, bf16[1,7168,512]{2,1,0:T(8,128)(2,1)} %param.13, s32[]{:T(128)S(6)} %select_n.17), kind=kOutput, calls=%fused_computation.1 | convolution fusion | flops 1882718208 | bytes 13893636 | tf_op jit(solution)/shard_map/dot_general | solution.py:122
  297.6 5.8 %add_convert_fusion.1 = bf16[1024,1792]{1,0:T(8,128)(2,1)S(1)} fusion(f32[1024,1792]{1,0:T(8,128)} %fusion.29, bf16[1024,512]{1,0:T(8,128)(2,1)S(1)} %copy-done.16, bf16[1,7168,512]{2,1,0:T(8,128)(2,1)} %param.13, s32[]{:T(128)S(6)} %select_n.18), kind=kOutput, calls=%fused_computation.2 | convolution fusion | flops 1882718208 | bytes 13893636 | tf_op jit(solution)/shard_map/dot_general | solution.py:122
  377.1 5.3 %collective-permute-done.108 = bf16[128,1792]{1,0:T(8,128)(2,1)S(1)} collective-permute-done((bf16[128,1792]{1,0:T(8,128)(2,1)S(1)}, bf16[128,1792]{1,0:T(8,128)(2,1)S(1)}, u32[]{:S(2)}, u32[]{:S(2)}) %collective-permute-start.108) | collective-permute-done | bytes 458784 | tf_op jit(solution)/shard_map/ppermute | solution.py:19
  (408 shorter events, 232.2 us)
Async XLA Ops:
  0.6 20.7 %collective-permute-start.9 = (bf16[128,1792]{1,0:T(8,128)(2,1)}, bf16[128,1792]{1,0:T(8,128)(2,1)S(1)}, u32[]{:S(2)}, u32[]{:S(2)}) collective-permute-start(bf16[128,1792]{1,0:T(8,128)(2,1)} %param.9), channel_id=1, source_target_pairs={{0,1},{1,2},{2,3},{3,0},{4,5},{5,6},{6,7},{7,4},{8,9},{9,10},{10,1... | collective-permute-start | bytes 1376264 | tf_op jit(solution)/shard_map/ppermute | solution.py:19
  6.7 36.7 %collective-permute-start.4 = (bf16[128,1792]{1,0:T(8,128)(2,1)}, bf16[128,1792]{1,0:T(8,128)(2,1)S(1)}, u32[]{:S(2)}, u32[]{:S(2)}) collective-permute-start(bf16[128,1792]{1,0:T(8,128)(2,1)} %param.9), channel_id=1, source_target_pairs={{0,4},{4,0},{8,12},{12,8},{16,20},{20,16},{24,28},{28,24},{1,5},{5... | collective-permute-start | bytes 1376264 | tf_op jit(solution)/shard_map/ppermute | solution.py:14
  21.4 26.0 %collective-permute-start.43 = (bf16[128,1792]{1,0:T(8,128)(2,1)}, bf16[128,1792]{1,0:T(8,128)(2,1)S(1)}, u32[]{:S(2)}, u32[]{:S(2)}) collective-permute-start(bf16[128,1792]{1,0:T(8,128)(2,1)} %param.8), channel_id=1, source_target_pairs={{0,4},{4,0},{8,12},{12,8},{16,20},{20,16},{24,28},{28,24},{1,5},{5... | collective-permute-start | bytes 1376264 | tf_op jit(solution)/shard_map/ppermute | solution.py:14
  47.3 43.3 %collective-permute-start.14 = (bf16[128,1792]{1,0:T(8,128)(2,1)S(1)}, bf16[128,1792]{1,0:T(8,128)(2,1)S(1)}, u32[]{:S(2)}, u32[]{:S(2)}) collective-permute-start(bf16[128,1792]{1,0:T(8,128)(2,1)S(1)} %collective-permute-done.9), channel_id=1, source_target_pairs={{0,4},{4,0},{8,12},{12,8},{16,20},{20,16},{24,28},{28,24},{1,5},{5... | collective-permute-start | bytes 1376264 | tf_op jit(solution)/shard_map/ppermute | solution.py:14
  55.4 26.1 %collective-permute-start.49 = (bf16[128,1792]{1,0:T(8,128)(2,1)S(1)}, bf16[128,1792]{1,0:T(8,128)(2,1)S(1)}, u32[]{:S(2)}, u32[]{:S(2)}) collective-permute-start(bf16[128,1792]{1,0:T(8,128)(2,1)S(1)} %collective-permute-done.48), channel_id=1, source_target_pairs={{0,8},{4,12},{8,0},{12,4},{16,24},{20,28},{24,16},{28,20},{1,9},{5... | collective-permute-start | bytes 1376264 | tf_op jit(solution)/shard_map/ppermute | solution.py:14
  56.7 30.7 %collective-permute-start.50 = (bf16[128,1792]{1,0:T(8,128)(2,1)S(1)}, bf16[128,1792]{1,0:T(8,128)(2,1)S(1)}, u32[]{:S(2)}, u32[]{:S(2)}) collective-permute-start(bf16[128,1792]{1,0:T(8,128)(2,1)S(1)} %collective-permute-done.48), channel_id=1, source_target_pairs={{0,16},{4,20},{8,24},{12,28},{16,0},{20,4},{24,8},{28,12},{1,17},{... | collective-permute-start | bytes 1376264 | tf_op jit(solution)/shard_map/ppermute | solution.py:14
  69.6 28.7 %collective-permute-start.53 = (bf16[128,1792]{1,0:T(8,128)(2,1)S(1)}, bf16[128,1792]{1,0:T(8,128)(2,1)S(1)}, u32[]{:S(2)}, u32[]{:S(2)}) collective-permute-start(bf16[128,1792]{1,0:T(8,128)(2,1)S(1)} %collective-permute-done.48), channel_id=1, source_target_pairs={{0,4},{4,0},{8,12},{12,8},{16,20},{20,16},{24,28},{28,24},{1,5},{5... | collective-permute-start | bytes 1376264 | tf_op jit(solution)/shard_map/ppermute | solution.py:14
  89.7 17.1 %collective-permute-start.20 = (bf16[128,1792]{1,0:T(8,128)(2,1)S(1)}, bf16[128,1792]{1,0:T(8,128)(2,1)S(1)}, u32[]{:S(2)}, u32[]{:S(2)}) collective-permute-start(bf16[128,1792]{1,0:T(8,128)(2,1)S(1)} %collective-permute-done.19), channel_id=1, source_target_pairs={{0,8},{4,12},{8,0},{12,4},{16,24},{20,28},{24,16},{28,20},{1,9},{5... | collective-permute-start | bytes 1376264 | tf_op jit(solution)/shard_map/ppermute | solution.py:14
  96.0 51.2 %collective-permute-start.24 = (bf16[128,1792]{1,0:T(8,128)(2,1)S(1)}, bf16[128,1792]{1,0:T(8,128)(2,1)S(1)}, u32[]{:S(2)}, u32[]{:S(2)}) collective-permute-start(bf16[128,1792]{1,0:T(8,128)(2,1)S(1)} %collective-permute-done.19), channel_id=1, source_target_pairs={{0,4},{4,0},{8,12},{12,8},{16,20},{20,16},{24,28},{28,24},{1,5},{5... | collective-permute-start | bytes 1376264 | tf_op jit(solution)/shard_map/ppermute | solution.py:14
  97.0 17.9 %collective-permute-start.59 = (bf16[128,1792]{1,0:T(8,128)(2,1)S(1)}, bf16[128,1792]{1,0:T(8,128)(2,1)S(1)}, u32[]{:S(2)}, u32[]{:S(2)}) collective-permute-start(bf16[128,1792]{1,0:T(8,128)(2,1)S(1)} %collective-permute-done.58), channel_id=1, source_target_pairs={{0,8},{4,12},{8,0},{12,4},{16,24},{20,28},{24,16},{28,20},{1,9},{5... | collective-permute-start | bytes 1376264 | tf_op jit(solution)/shard_map/ppermute | solution.py:14
  98.3 23.4 %collective-permute-start.15 = (bf16[128,1792]{1,0:T(8,128)(2,1)S(1)}, bf16[128,1792]{1,0:T(8,128)(2,1)S(1)}, u32[]{:S(2)}, u32[]{:S(2)}) collective-permute-start(bf16[128,1792]{1,0:T(8,128)(2,1)S(1)} %collective-permute-done.10), channel_id=1, source_target_pairs={{0,4},{4,0},{8,12},{12,8},{16,20},{20,16},{24,28},{28,24},{1,5},{5... | collective-permute-start | bytes 1376264 | tf_op jit(solution)/shard_map/ppermute | solution.py:14
  114.9 24.1 %collective-permute-start.60 = (bf16[128,1792]{1,0:T(8,128)(2,1)S(1)}, bf16[128,1792]{1,0:T(8,128)(2,1)S(1)}, u32[]{:S(2)}, u32[]{:S(2)}) collective-permute-start(bf16[128,1792]{1,0:T(8,128)(2,1)S(1)} %collective-permute-done.58), channel_id=1, source_target_pairs={{0,16},{4,20},{8,24},{12,28},{16,0},{20,4},{24,8},{28,12},{1,17},{... | collective-permute-start | bytes 1376264 | tf_op jit(solution)/shard_map/ppermute | solution.py:14
  121.7 32.7 %collective-permute-start.63 = (bf16[128,1792]{1,0:T(8,128)(2,1)S(1)}, bf16[128,1792]{1,0:T(8,128)(2,1)S(1)}, u32[]{:S(2)}, u32[]{:S(2)}) collective-permute-start(bf16[128,1792]{1,0:T(8,128)(2,1)S(1)} %collective-permute-done.58), channel_id=1, source_target_pairs={{0,4},{4,0},{8,12},{12,8},{16,20},{20,16},{24,28},{28,24},{1,5},{5... | collective-permute-start | bytes 1376264 | tf_op jit(solution)/shard_map/ppermute | solution.py:14
  126.2 18.9 %collective-permute-start.68 = (bf16[128,1792]{1,0:T(8,128)(2,1)S(1)}, bf16[128,1792]{1,0:T(8,128)(2,1)S(1)}, u32[]{:S(2)}, u32[]{:S(2)}) collective-permute-start(bf16[128,1792]{1,0:T(8,128)(2,1)S(1)} %collective-permute-done.58), channel_id=1, source_target_pairs={{0,1},{1,2},{2,3},{3,0},{4,5},{5,6},{6,7},{7,4},{8,9},{9,10},{10,1... | collective-permute-start | bytes 1376264 | tf_op jit(solution)/shard_map/ppermute | solution.py:19
  147.1 17.5 %collective-permute-start.25 = (bf16[128,1792]{1,0:T(8,128)(2,1)S(1)}, bf16[128,1792]{1,0:T(8,128)(2,1)S(1)}, u32[]{:S(2)}, u32[]{:S(2)}) collective-permute-start(bf16[128,1792]{1,0:T(8,128)(2,1)S(1)} %collective-permute-done.20), channel_id=1, source_target_pairs={{0,4},{4,0},{8,12},{12,8},{16,20},{20,16},{24,28},{28,24},{1,5},{5... | collective-permute-start | bytes 1376264 | tf_op jit(solution)/shard_map/ppermute | solution.py:14
  147.2 18.6 %collective-permute-start.26 = (bf16[128,1792]{1,0:T(8,128)(2,1)S(1)}, bf16[128,1792]{1,0:T(8,128)(2,1)S(1)}, u32[]{:S(2)}, u32[]{:S(2)}) collective-permute-start(bf16[128,1792]{1,0:T(8,128)(2,1)S(1)} %collective-permute-done.21), channel_id=1, source_target_pairs={{0,4},{4,0},{8,12},{12,8},{16,20},{20,16},{24,28},{28,24},{1,5},{5... | collective-permute-start | bytes 1376264 | tf_op jit(solution)/shard_map/ppermute | solution.py:14
  154.4 38.0 %collective-permute-start.34 = (bf16[128,1792]{1,0:T(8,128)(2,1)S(1)}, bf16[128,1792]{1,0:T(8,128)(2,1)S(1)}, u32[]{:S(2)}, u32[]{:S(2)}) collective-permute-start(bf16[128,1792]{1,0:T(8,128)(2,1)S(1)} %collective-permute-done.29), channel_id=1, source_target_pairs={{0,4},{4,0},{8,12},{12,8},{16,20},{20,16},{24,28},{28,24},{1,5},{5... | collective-permute-start | bytes 1376264 | tf_op jit(solution)/shard_map/ppermute | solution.py:14
  164.5 19.5 %collective-permute-start.69 = (bf16[128,1792]{1,0:T(8,128)(2,1)S(1)}, bf16[128,1792]{1,0:T(8,128)(2,1)S(1)}, u32[]{:S(2)}, u32[]{:S(2)}) collective-permute-start(bf16[128,1792]{1,0:T(8,128)(2,1)S(1)} %collective-permute-done.68), channel_id=1, source_target_pairs={{0,8},{4,12},{8,0},{12,4},{16,24},{20,28},{24,16},{28,20},{1,9},{5... | collective-permute-start | bytes 1376264 | tf_op jit(solution)/shard_map/ppermute | solution.py:14
  168.8 21.1 %collective-permute-start.70 = (bf16[128,1792]{1,0:T(8,128)(2,1)S(1)}, bf16[128,1792]{1,0:T(8,128)(2,1)S(1)}, u32[]{:S(2)}, u32[]{:S(2)}) collective-permute-start(bf16[128,1792]{1,0:T(8,128)(2,1)S(1)} %collective-permute-done.68), channel_id=1, source_target_pairs={{0,16},{4,20},{8,24},{12,28},{16,0},{20,4},{24,8},{28,12},{1,17},{... | collective-permute-start | bytes 1376264 | tf_op jit(solution)/shard_map/ppermute | solution.py:14
  169.9 28.2 %collective-permute-start.73 = (bf16[128,1792]{1,0:T(8,128)(2,1)S(1)}, bf16[128,1792]{1,0:T(8,128)(2,1)S(1)}, u32[]{:S(2)}, u32[]{:S(2)}) collective-permute-start(bf16[128,1792]{1,0:T(8,128)(2,1)S(1)} %collective-permute-done.68), channel_id=1, source_target_pairs={{0,4},{4,0},{8,12},{12,8},{16,20},{20,16},{24,28},{28,24},{1,5},{5... | collective-permute-start | bytes 1376264 | tf_op jit(solution)/shard_map/ppermute | solution.py:14
  282.7 34.5 %collective-permute-start.78 = (bf16[512,1792]{1,0:T(8,128)(2,1)}, bf16[512,1792]{1,0:T(8,128)(2,1)}, u32[]{:S(2)}, u32[]{:S(2)}) collective-permute-start(bf16[512,1792]{1,0:T(8,128)(2,1)} %slice.231), channel_id=1, source_target_pairs={{0,4},{4,0},{8,12},{12,8},{16,20},{20,16},{24,28},{28,24},{1,5},{5... | collective-permute-start | bytes 5505032 | tf_op jit(solution)/shard_map/ppermute | solution.py:14
  287.8 20.7 %collective-permute-start.85 = (bf16[512,1792]{1,0:T(8,128)(2,1)}, bf16[512,1792]{1,0:T(8,128)(2,1)}, u32[]{:S(2)}, u32[]{:S(2)}) collective-permute-start(bf16[512,1792]{1,0:T(8,128)(2,1)} %slice.240), channel_id=1, source_target_pairs={{0,4},{4,0},{8,12},{12,8},{16,20},{20,16},{24,28},{28,24},{1,5},{5... | collective-permute-start | bytes 5505032 | tf_op jit(solution)/shard_map/ppermute | solution.py:14
  295.4 17.6 %collective-permute-start.99 = (bf16[512,1792]{1,0:T(8,128)(2,1)}, bf16[512,1792]{1,0:T(8,128)(2,1)}, u32[]{:S(2)}, u32[]{:S(2)}) collective-permute-start(bf16[512,1792]{1,0:T(8,128)(2,1)} %slice.258), channel_id=1, source_target_pairs={{0,4},{4,0},{8,12},{12,8},{16,20},{20,16},{24,28},{28,24},{1,5},{5... | collective-permute-start | bytes 5505032 | tf_op jit(solution)/shard_map/ppermute | solution.py:14
  311.9 29.5 %collective-permute-start.87 = (bf16[64,1792]{1,0:T(8,128)(2,1)S(1)}, bf16[64,1792]{1,0:T(8,128)(2,1)S(1)}, u32[]{:S(2)}, u32[]{:S(2)}) collective-permute-start(bf16[64,1792]{1,0:T(8,128)(2,1)S(1)} %get-tuple-element.17), channel_id=1, source_target_pairs={{0,16},{4,20},{8,24},{12,28},{16,0},{20,4},{24,8},{28,12},{1,17},{... | collective-permute-start | bytes 688136 | tf_op jit(solution)/shard_map/ppermute | solution.py:14
  (113 other events, 1088.5 us)

commit v2 on v0

v2 whole, which is shorter than its diff:
```python
import functools

import jax
import jax.numpy as jnp
from jax import lax
from jax.experimental import pallas as pl
from jax.experimental.pallas import tpu as pltpu
from jax.sharding import PartitionSpec as P

BF16 = jnp.bfloat16
F32 = jnp.float32
LAST = (((1,), (1,)), ((), ()))
FIRST = (((0,), (0,)), ((), ()))
PLAIN = (((1,), (0,)), ((), ()))

dot = functools.partial(lax.dot_general, preferred_element_type=F32)


def after(a, *others):
    return lax.optimization_barrier((a,) + others)[0]


def swap(a, mask):
    n = lax.axis_size("expert")
    return lax.ppermute(a, "expert", [(i, i ^ mask) for i in range(n)])


def ring(a):
    n = lax.axis_size("tensor")
    return lax.ppermute(a, "tensor", [(i, (i + 1) % n) for i in range(n)])


class Links:
    def __init__(self):
        self.held, self.now = [], []

    def turn(self, *work):
        self.held, self.now = self.now + list(work), []

    def send(self, link, a):
        if self.held:
            a = after(a, *self.held)
        self.now.append(ring(a) if link == 0 else swap(a, link))
        return self.now[-1]


def far_masks():
    n = lax.axis_size("expert")
    return [1 << b for b in range(1, n.bit_length() - 1)]


def stack(refs, places, rows):
    return jnp.concatenate([refs[i][at : at + rows, :] for i, at in places], axis=0)


def chunk_of(width, most):
    return max(c for c in range(128, most + 1, 128) if width % c == 0)


def spec(shape, index):
    return pl.BlockSpec(shape, index)


def fixed(a):
    return pl.BlockSpec(a.shape, lambda k, s: (0,) * a.ndim)


def call(kernel, name, at, grid, ins, in_specs, outs, out_specs, scratch=(), aliases=None, flops=0):
    moved = sum(a.size * a.dtype.itemsize for a in ins) + sum(
        o.size * o.dtype.itemsize for o in outs
    )
    return pl.pallas_call(
        kernel,
        out_shape=outs,
        grid_spec=pltpu.PrefetchScalarGridSpec(
            num_scalar_prefetch=1,
            grid=(grid,),
            in_specs=in_specs,
            out_specs=out_specs,
            scratch_shapes=list(scratch),
        ),
        input_output_aliases=aliases or {},
        compiler_params=pltpu.CompilerParams(
            dimension_semantics=("arbitrary",), vmem_limit_bytes=48 * 2**20
        ),
        cost_estimate=pl.CostEstimate(flops=flops, bytes_accessed=moved, transcendentals=0),
        name=name,
    )(at, *ins)


def forward(at, parts, rows, weight, wg, wu, wd, sums, final):
    arrays, tok, grd = parts
    n, (width, ff), count = len(arrays), (arrays[0].shape[1], wg.shape[1]), len(tok) * rows
    ck = chunk_of(width, 896)
    steps = width // ck

    def kernel(_, *refs):
        xs, (w_ref, g_ref, u_ref, d_ref) = refs[:n], refs[n : n + 4]
        rest = refs[n + 4 :]
        before = rest[: len(sums)]
        outs = rest[len(sums) :]
        accs = outs[3:] if final else outs
        k = pl.program_id(0)

        @pl.when(k == 0)
        def _():
            for i, acc in enumerate(accs):
                acc[...] = before[i][...] if sums else jnp.zeros_like(acc)

        x = stack(xs, tok, rows)
        accs[0][...] += dot(x, g_ref[...], PLAIN)
        accs[1][...] += dot(x, u_ref[...], PLAIN)
        g = (w_ref[...] * stack(xs, grd, rows).astype(F32)).astype(BF16)
        accs[2][...] += dot(g, d_ref[...], LAST)
        if final:

            @pl.when(k == steps - 1)
            def _():
                def piece(i, _):
                    at = pl.ds(pl.multiple_of(i * rows, rows), rows)
                    gate, upper, dh = accs[0][at, :], accs[1][at, :], accs[2][at, :]
                    sig = jax.nn.sigmoid(gate)
                    act = gate * sig
                    outs[0][at, :] = (act * upper).astype(BF16)
                    outs[1][at, :] = (dh * upper * sig * (1.0 + gate * (1.0 - sig))).astype(BF16)
                    outs[2][at, :] = (dh * act).astype(BF16)
                    return _

                lax.fori_loop(0, count // rows, piece, 0)

    out = jax.ShapeDtypeStruct((count, ff), BF16 if final else F32)
    in_specs = [spec((a.shape[0], ck), lambda k, s: (0, k)) for a in arrays] + [
        fixed(weight),
        spec((ck, ff), lambda k, s: (s[0] * steps + k, 0)),
        spec((ck, ff), lambda k, s: (s[0] * steps + k, 0)),
        spec((ff, ck), lambda k, s: (0, s[0] * steps + k)),
    ]
    in_specs += [fixed(a) for a in sums]
    return call(
        kernel, "forward", at, steps, [*arrays, weight, wg, wu, wd, *sums], in_specs,
        [out] * 3, [fixed(out)] * 3,
        scratch=[pltpu.VMEM((count, ff), F32)] * 3 if final else (),
        flops=6 * count * width * ff,
    )


def inputs_back(at, dgate, dup, wg, wu, width):
    count, ff = dgate.shape
    ck = chunk_of(width, 256)
    steps = width // ck
    half = count // 2

    def kernel(_, a_ref, b_ref, g_ref, u_ref, mine_ref, near_ref):
        for lo, out in ((half, near_ref), (0, mine_ref)):
            part = dot(a_ref[lo : lo + half, :], g_ref[...], LAST)
            part += dot(b_ref[lo : lo + half, :], u_ref[...], LAST)
            out[...] = part.astype(BF16)

    out = jax.ShapeDtypeStruct((half, width), BF16)
    weights = spec((ck, ff), lambda k, s: (s[0] * steps + k, 0))
    return call(
        kernel, "inputs_back", at, steps, [dgate, dup, wg, wu],
        [fixed(dgate), fixed(dup), weights, weights],
        [out] * 2, [spec((half, ck), lambda k, s: (0, k))] * 2,
        flops=4 * count * width * ff,
    )


def weights_back(at, parts, rows, weight, hidden, dgate, dup, shapes, grads):
    arrays, tok, grd = parts
    n, width, (count, ff) = len(arrays), arrays[0].shape[1], hidden.shape
    ck = chunk_of(width, 256)
    steps = width // ck

    def kernel(_, *refs):
        xs, (w_ref, h_ref, a_ref, b_ref) = refs[:n], refs[n : n + 4]
        wg_ref, wu_ref, wd_ref = refs[-3:]
        x = stack(xs, tok, rows)
        wg_ref[...] = dot(x, a_ref[...], FIRST).astype(BF16)
        wu_ref[...] = dot(x, b_ref[...], FIRST).astype(BF16)
        g = (w_ref[...] * stack(xs, grd, rows).astype(F32)).astype(BF16)
        wd_ref[...] = dot(h_ref[...], g, FIRST).astype(BF16)

    in_specs = [spec((a.shape[0], ck), lambda k, s: (0, k)) for a in arrays]
    in_specs += [fixed(weight), fixed(hidden), fixed(dgate), fixed(dup)]
    in_specs += [pl.BlockSpec(memory_space=pl.ANY)] * len(grads)
    return call(
        kernel, "weights_back", at, steps, [*arrays, weight, hidden, dgate, dup, *grads], in_specs,
        [jax.ShapeDtypeStruct(s, BF16) for s in shapes],
        [
            spec((ck, ff), lambda k, s: (s[0] * steps + k, 0)),
            spec((ck, ff), lambda k, s: (s[0] * steps + k, 0)),
            spec((ff, ck), lambda k, s: (0, s[0] * steps + k)),
        ],
        aliases={n + 5 + i: i for i in range(len(grads))},
        flops=6 * count * width * ff,
    )


def gather_both(links, both, table, use):
    X, Y = far_masks()
    shards = lax.axis_size("tensor")
    rows = both.shape[0] // 2
    hop, xs, ys, ds, near = {0: both}, {}, {}, {}, {}
    tables, work = [table], ()
    for r in range(shards + 2):
        if r < shards - 1:
            hop[r + 1] = links.send(0, hop[r])
        if r < shards:
            xs[r] = links.send(X, hop[r])
            ys[r] = links.send(Y, hop[r])
        if r == 0:
            tables += [links.send(X, table), links.send(Y, table)]
        if r == 1:
            tables.append(links.send(Y, tables[1]))
        if r == 2:
            tables += [links.send(1, t) for t in tables]
        if 1 <= r <= shards:
            q = r - 1
            ds[q] = [links.send(Y, xs[q][:rows]), links.send(X, ys[q][rows:])]
            near[q] = [links.send(1, a) for a in (hop[q], xs[q], ys[q])]
        if 2 <= r <= shards + 1:
            q = r - 2
            near[q] += [links.send(1, a) for a in ds[q]]
            arrays = [hop[q], xs[q], ys[q]] + ds[q] + near[q]
            tok = [(0, 0), (1, 0), (2, 0), (3, 0), (5, 0), (6, 0), (7, 0), (8, 0)]
            grd = [(0, rows), (1, rows), (2, rows), (4, 0), (5, rows), (6, rows), (7, rows), (9, 0)]
            work = use(q, (arrays, tok, grd), tables)
        links.turn(*work)


def gather_plain(own, table, use):
    rows = own.shape[0] // 2
    tables = [table]
    for m in far_masks() + [1]:
        tables = tables + [swap(t, m) for t in tables]
    for j in range(lax.axis_size("tensor")):
        own = ring(own) if j else own
        pieces = [own]
        for m in far_masks() + [1]:
            pieces = pieces + [swap(p, m) for p in pieces]
        places = range(len(pieces))
        use(j, (pieces, [(i, 0) for i in places], [(i, rows) for i in places]), tables)


def plus(*terms):
    return functools.reduce(lambda a, b: a + b, [t.astype(F32) for t in terms]).astype(BF16)


def on_device(tokens, grad_out, expert_ids, gates, w_gate, w_up, w_down):
    owners, shards = lax.axis_size("expert"), lax.axis_size("tensor")
    me, z = lax.axis_index("expert"), lax.axis_index("tensor")
    rows, width = tokens.shape
    wg, wu, wd = w_gate[0], w_up[0], w_down[0]
    far = far_masks()

    chosen = expert_ids[:, :, None] == jnp.arange(owners, dtype=jnp.int32)
    table = jnp.sum(jnp.where(chosen, gates[:, :, None], 0.0), axis=1).T
    at = [lax.rem(z - j + shards, shards).reshape(1) for j in range(shards)]
    both = jnp.concatenate([tokens, grad_out])
    kept, state = [], {"sums": ()}

    def use(j, parts, tables):
        if j == 0:
            w = [lax.dynamic_index_in_dim(t, me, 0, False) for t in tables]
            state["weight"] = jnp.stack(w).reshape(-1, 1)
        kept.append(parts)
        state["sums"] = forward(
            at[j], parts, rows, state["weight"], wg, wu, wd, state["sums"], j == shards - 1
        )
        return state["sums"]

    links = Links()
    if len(far) == 2:
        gather_both(links, both, table, use)
    else:
        gather_plain(both, table, use)
    hidden, dgate, dup = state["sums"]

    order = list(range(1, shards)) + [0]
    grads = ()

    def grads_of(i, *first):
        late = [after(a, *first) for a in (hidden, dgate, dup)]
        return weights_back(
            at[i], kept[i], rows, state["weight"], *late, (wg.shape, wu.shape, wd.shape), grads
        )

    back = lambda j, *first: inputs_back(at[j], after(dgate, *first) if first else dgate, dup, wg, wu, width)
    if len(far) == 2:
        X, Y = far
        links = Links()
        n = shards
        parts, got, mine, one, two, acc, hops = {}, {}, {}, {}, {}, {}, {}
        parts[0] = back(order[0])
        done = 0
        for r in range(1, n + 4):
            if 0 <= r - 4 < n - 1:
                hops[r - 4] = links.send(0, acc[r - 4])
            if 0 <= r - 3 < n:
                q = r - 3
                m = mine[q]
                north = plus(m[2, :h], one[q][0]), m[2, h:]
                east = m[1, :h], plus(m[1, h:], one[q][1])
                two[q] = [
                    links.send(X, jnp.concatenate(east)),
                    links.send(Y, jnp.concatenate(north)),
                ]
            if 0 <= r - 2 < n:
                q = r - 2
                mine[q] = plus(parts[q][0], got[q]).reshape(-1, rows, width)
                h = rows // 2
                one[q] = [links.send(X, mine[q][3, :h]), links.send(Y, mine[q][3, h:])]
            if 0 <= r - 1 < n:
                got[r - 1] = links.send(1, parts[r - 1][1])
            last = [a for a in links.held if a.size > 1]
            if r < n:
                parts[r] = back(order[r], *last)
                links.turn(*parts[r])
            elif done < shards:
                grads = grads_of(done, *last)
                done += 1
                links.turn(*grads)
            if 0 <= r - 3 < n:
                q = r - 3
                terms = [mine[q][0], *two[q]] + ([hops[q - 1]] if q else [])
                acc[q] = plus(*terms)
        result = acc[n - 1]
        while done < shards:
            grads = grads_of(done)
            done += 1
    else:
        result = None
        for j in order:
            mine, near = back(j)
            mine = plus(mine, swap(near, 1)).reshape(-1, rows, width)
            for m in reversed(far):
                cut = mine.shape[0] // 2
                mine = plus(mine[:cut], swap(mine[cut:], m))
            terms = [mine[0]] if result is None else [mine[0], ring(result)]
            result = plus(*terms)
        for j in range(shards):
            grads = grads_of(j)
    return (result, grads[0][None], grads[1][None], grads[2][None])


def solution(mesh):
    placed = (
        P("expert", "tensor"),
        P("expert", "tensor"),
        P("expert", None),
        P("expert", None),
        P("expert", None, "tensor"),
        P("expert", None, "tensor"),
        P("expert", "tensor", None),
    )
    return jax.shard_map(
        on_device,
        mesh=mesh,
        in_specs=placed,
        out_specs=(
            P("expert", "tensor"),
            P("expert", None, "tensor"),
            P("expert", None, "tensor"),
            P("expert", "tensor", None),
        ),
        check_vma=False,
    )
```

time: 610 us -> 319 us (0.52); the launches traced: 602 us -> 317 us
  waiting for transfers between devices: 439 us -> 93.7 us
  Pallas kernels: 0 us -> 129 us
  matrix products: 77.9 us -> 0 us
  starting transfers between devices: 15.4 us -> 53.3 us
  local copies, waits for them, and re-layouts: 48.2 us -> 24.3 us
  between operations: 14.3 us -> 1.51 us
  other arithmetic: 7.01 us -> 14.8 us
    reduce_scatter x1 -> x0, waiting for transfers between devices: 243 us -> none  [on_device(): lax.psum_scatter(partial_dx, 'tensor', scatter_dimension=1, tiled=True)]
    pallas_call x0 -> x12, Pallas kernels: none -> 129 us  [call(): pl.pallas_call(kernel, out_shape=outs, grid_spec=pltpu.PrefetchScalarGrid...]
    all_gather x2 -> x0, waiting for transfers between devices: 115 us -> none  [the longest x1 71.7 us: on_device(): lax.all_gather(weighted, 'tensor', axis=1, tiled=True)]
    ppermute x0 -> x69, waiting for transfers between devices: none -> 93.7 us  [the longest x63 87.9 us: swap(): return lax.ppermute(a, 'expert', [(i, i ^ mask) for i in range(n)])]
    all_to_all x3 -> x0, waiting for transfers between devices: 81 us -> none  [the longest x1 65.2 us: on_device(): lax.all_to_all(send_grads, 'expert', split_axis=0, concat_axis=0, tiled=T...]
    dot_general x8 -> x0, matrix products: 77.9 us -> none  [the longest x1 12.5 us: on_device(): lax.dot_general(dup, wu, contract_last, preferred_element_type=jnp.float32)]
    ppermute x0 -> x69, starting transfers between devices: none -> 53.3 us  [the longest x63 41.9 us: swap(): return lax.ppermute(a, 'expert', [(i, i ^ mask) for i in range(n)])]
    scatter x2 -> x0, local copies, waits for them, and re-layouts: 22.3 us -> none  [the longest x1 11.1 us: on_device(): send_rows = empty.at[position].set(jnp.repeat(whole_tok, top_count, axis=0))]
  transfers between devices with their start and end apart: 6 -> 69, of which waited for: 5 -> 15; matrix products, arithmetic and copies ran while one was open for 11% -> 6% of each run, Pallas kernels for 0% -> 30%
where the time goes in v2:
time: 319 us; the launch traced here: 317 us
  Pallas kernels  129 us (40%)
  waiting for transfers between devices  93.7 us (29%)
  starting transfers between devices  53.3 us (17%)
  local copies, waits for them, and re-layouts  24.3 us (8%)
  other arithmetic  14.8 us (5%)
    pallas_call x12, Pallas kernels, call(): pl.pallas_call(kernel, out_shape=outs, grid_spec=pltpu.PrefetchScalarGrid...  129 us
    ppermute x63, waiting for transfers between devices, swap(): return lax.ppermute(a, 'expert', [(i, i ^ mask) for i in range(n)])  87.9 us
    ppermute x63, starting transfers between devices, swap(): return lax.ppermute(a, 'expert', [(i, i ^ mask) for i in range(n)])  41.9 us
    unnamed x69, local copies, waits for them, and re-layouts  17.1 us
    convert_element_type x12, other arithmetic, plus(): functools.reduce(lambda a, b: a + b, [t.astype(F32) for t in terms])  14.5 us
    ppermute x6, starting transfers between devices, ring(): return lax.ppermute(a, 'tensor', [(i, (i + 1) % n) for i in range(n)])  11.5 us
  transfers between devices with their start and end apart: 69, of which 15 were waited for; matrix products, arithmetic and copies ran while one was open for 6% of the time, Pallas kernels for 30%

profile of v2, /device:TPU:0, one launch (start us, length us, event | category | flops | bytes accessed | tf_op | source)
XLA Modules:
  0.0 317.1 jit_solution(15006602443693279038)
XLA Ops:
  2.8 3.1 collective-permute-start
  10.0 17.8 %collective-permute-done.3 = f32[8,128]{1,0:T(8,128)S(1)} collective-permute-done((f32[8,128]{1,0:T(8,128)S(1)}, f32[8,128]{1,0:T(8,128)S(1)}, u32[]{:S(2)}, u32[]{:S(2)}) %collective-permute-start.3) | collective-permute-done | bytes 4128 | tf_op jit(solution)/shard_map/ppermute | solution.py:25
  34.9 6.5 %collective-permute-done.8 = f32[8,128]{1,0:T(8,128)S(1)} collective-permute-done((f32[8,128]{1,0:T(8,128)S(1)}, f32[8,128]{1,0:T(8,128)S(1)}, u32[]{:S(2)}, u32[]{:S(2)}) %collective-permute-start.8) | collective-permute-done | bytes 4128 | tf_op jit(solution)/shard_map/ppermute | solution.py:25
  42.9 3.0 collective-permute-done.10.refs_4_
  45.9 5.8 %collective-permute-done.5.refs_0_ = bf16[256,1792]{1,0:T(8,128)(2,1)} collective-permute-done((bf16[256,1792]{1,0:T(8,128)(2,1)S(1)}, bf16[256,1792]{1,0:T(8,128)(2,1)}, u32[]{:S(2)}, u32[]{:S(2)}) %collective-permute-start.5) | collective-permute-done | bytes 917536 | tf_op jit(solution)/shard_map/ppermute | solution.py:30
  51.8 10.5 %collective-permute-done.6.refs_1_ = bf16[256,1792]{1,0:T(8,128)(2,1)S(1)} collective-permute-done((bf16[256,1792]{1,0:T(8,128)(2,1)S(1)}, bf16[256,1792]{1,0:T(8,128)(2,1)S(1)}, u32[]{:S(2)}, u32[]{:S(2)}) %collective-permute-start.6) | collective-permute-done | bytes 917536 | tf_op jit(solution)/shard_map/ppermute | solution.py:25
  70.0 10.5 %collective-permute-done.21.refs_3_ = bf16[128,1792]{1,0:T(8,128)(2,1)S(1)} collective-permute-done((bf16[128,1792]{1,0:T(8,128)(2,1)}, bf16[128,1792]{1,0:T(8,128)(2,1)S(1)}, u32[]{:S(2)}, u32[]{:S(2)}) %collective-permute-start.21) | collective-permute-done | bytes 458784 | tf_op jit(solution)/shard_map/ppermute | solution.py:25
  82.0 11.4 %collective-permute-done.22.refs_4_ = bf16[128,1792]{1,0:T(8,128)(2,1)} collective-permute-done((bf16[128,1792]{1,0:T(8,128)(2,1)}, bf16[128,1792]{1,0:T(8,128)(2,1)}, u32[]{:S(2)}, u32[]{:S(2)}) %collective-permute-start.22) | collective-permute-done | bytes 458784 | tf_op jit(solution)/shard_map/ppermute | solution.py:25
  99.6 12.3 %forward.4 = (f32[1024,512]{1,0:T(8,128)}, f32[1024,512]{1,0:T(8,128)}, f32[1024,512]{1,0:T(8,128)}) custom-call(s32[1]{0:T(128)} %bitcast._, bf16[256,1792]{1,0:T(8,128)(2,1)S(1)} %copy-done.12, bf16[256,1792]{1,0:T(8,128)(2,1)S(1)} %copy-done.6, bf16[256,1792]{1,0:T(8,128)(2,1)S(1)} %copy-done.9, bf16[128,1792]{1,0:T(8,128)(2,1)} %collective-permute-done.9.refs_3_, ...), custom_call_target="tpu_custom_call" | custom-call | flops 5637144576 | bytes 35655680 | tf_op jit(solution)/shard_map/forward/pallas_call | solution.py:72
  117.3 7.8 %collective-permute-done.30.refs_3_ = bf16[128,1792]{1,0:T(8,128)(2,1)} collective-permute-done((bf16[128,1792]{1,0:T(8,128)(2,1)S(1)}, bf16[128,1792]{1,0:T(8,128)(2,1)}, u32[]{:S(2)}, u32[]{:S(2)}) %collective-permute-start.30) | collective-permute-done | bytes 458784 | tf_op jit(solution)/shard_map/ppermute | solution.py:25
  134.5 14.1 %forward.5 = (f32[1024,512]{1,0:T(8,128)}, f32[1024,512]{1,0:T(8,128)}, f32[1024,512]{1,0:T(8,128)}) custom-call(s32[1]{0:T(128)} %bitcast.8._, bf16[256,1792]{1,0:T(8,128)(2,1)S(1)} %copy-done.3, bf16[256,1792]{1,0:T(8,128)(2,1)S(1)} %collective-permute-done.6.refs_1_, bf16[256,1792]{1,0:T(8,128)(2,1)S(1)} %collective-permute-done.7.refs_2_, ...), custom_call_target="tpu_custom_call" | custom-call | flops 5637144576 | bytes 41947136 | tf_op jit(solution)/shard_map/forward/pallas_call | solution.py:72
  153.6 14.5 %forward.6 = (f32[1024,512]{1,0:T(8,128)}, f32[1024,512]{1,0:T(8,128)}, f32[1024,512]{1,0:T(8,128)}) custom-call(s32[1]{0:T(128)} %bitcast.9._, bf16[256,1792]{1,0:T(8,128)(2,1)} %collective-permute-done.5.refs_0_, bf16[256,1792]{1,0:T(8,128)(2,1)S(1)} %collective-permute-done.15.refs_1_, bf16[256,1792]{1,0:T(8,128)(2,1)} %collective-permute-done.16.refs_2_, ...), custom_call_target="tpu_custom_call" | custom-call | flops 5637144576 | bytes 41947136 | tf_op jit(solution)/shard_map/forward/pallas_call | solution.py:72
  171.0 15.3 %forward.7 = (bf16[1024,512]{1,0:T(8,128)(2,1)}, bf16[1024,512]{1,0:T(8,128)(2,1)}, bf16[1024,512]{1,0:T(8,128)(2,1)}) custom-call(s32[1]{0:T(128)} %bitcast.1._, bf16[256,1792]{1,0:T(8,128)(2,1)} %collective-permute-done.14.refs_0_, bf16[256,1792]{1,0:T(8,128)(2,1)} %collective-permute-done.28.refs_1_, bf16[256,1792]{1,0:T(8,128)(2,1)} %collective-permute-done.29.refs_2_, ...), custom_call_target="tpu_custom_call" | custom-call | flops 5637144576 | bytes 38801408 | tf_op jit(solution)/shard_map/forward/pallas_call | solution.py:72
  188.7 7.3 %inputs_back.4 = (bf16[512,1792]{1,0:T(8,128)(2,1)S(1)}, bf16[512,1792]{1,0:T(8,128)(2,1)S(1)}) custom-call(s32[1]{0:T(128)} %bitcast.8._, bf16[1024,512]{1,0:T(8,128)(2,1)S(1)} %copy-done, bf16[1024,512]{1,0:T(8,128)(2,1)S(1)} %copy-done.1, bf16[7168,512]{1,0:T(8,128)(2,1)} %bitcast.94, bf16[7168,512]{1,0:T(8,128)(2,1)} %bitcast.102), custom_call_target="tpu_custom_call" | custom-call | flops 3758096384 | bytes 20447232 | tf_op jit(solution)/shard_map/inputs_back/pallas_call | solution.py:72
  196.2 7.3 %inputs_back.5 = (bf16[512,1792]{1,0:T(8,128)(2,1)S(1)}, bf16[512,1792]{1,0:T(8,128)(2,1)S(1)}) custom-call(s32[1]{0:T(128)} %bitcast.9._, bf16[1024,512]{1,0:T(8,128)(2,1)S(1)} %copy-done, bf16[1024,512]{1,0:T(8,128)(2,1)S(1)} %copy-done.1, bf16[7168,512]{1,0:T(8,128)(2,1)} %bitcast.95, bf16[7168,512]{1,0:T(8,128)(2,1)} %bitcast.103), custom_call_target="tpu_custom_call" | custom-call | flops 3758096384 | bytes 20447232 | tf_op jit(solution)/shard_map/inputs_back/pallas_call | solution.py:72
  209.8 7.3 %inputs_back.6 = (bf16[512,1792]{1,0:T(8,128)(2,1)S(1)}, bf16[512,1792]{1,0:T(8,128)(2,1)S(1)}) custom-call(s32[1]{0:T(128)} %bitcast.1._, bf16[1024,512]{1,0:T(8,128)(2,1)S(1)} %copy-done, bf16[1024,512]{1,0:T(8,128)(2,1)S(1)} %copy-done.1, bf16[7168,512]{1,0:T(8,128)(2,1)} %bitcast.96, bf16[7168,512]{1,0:T(8,128)(2,1)} %bitcast.104), custom_call_target="tpu_custom_call" | custom-call | flops 3758096384 | bytes 20447232 | tf_op jit(solution)/shard_map/inputs_back/pallas_call | solution.py:72
  223.5 7.3 %inputs_back.7 = (bf16[512,1792]{1,0:T(8,128)(2,1)S(1)}, bf16[512,1792]{1,0:T(8,128)(2,1)S(1)}) custom-call(s32[1]{0:T(128)} %bitcast._, bf16[1024,512]{1,0:T(8,128)(2,1)S(1)} %copy-done, bf16[1024,512]{1,0:T(8,128)(2,1)S(1)} %copy-done.1, bf16[7168,512]{1,0:T(8,128)(2,1)} %bitcast.97, bf16[7168,512]{1,0:T(8,128)(2,1)} %bitcast.105), custom_call_target="tpu_custom_call" | custom-call | flops 3758096384 | bytes 20447232 | tf_op jit(solution)/shard_map/inputs_back/pallas_call | solution.py:72
  230.8 4.1 %collective-permute-done.52 = bf16[64,1792]{1,0:T(8,128)(2,1)} collective-permute-done((bf16[64,1792]{1,0:T(8,128)(2,1)S(1)}, bf16[64,1792]{1,0:T(8,128)(2,1)}, u32[]{:S(2)}, u32[]{:S(2)}) %collective-permute-start.52) | collective-permute-done | bytes 229408 | tf_op jit(solution)/shard_map/ppermute | solution.py:25
  244.8 10.8 %weights_back.4 = (bf16[7168,512]{1,0:T(8,128)(2,1)}, bf16[7168,512]{1,0:T(8,128)(2,1)}, bf16[512,7168]{1,0:T(8,128)(2,1)}) custom-call(s32[1]{0:T(128)} %bitcast._, bf16[256,1792]{1,0:T(8,128)(2,1)S(1)} %copy-done.13, bf16[256,1792]{1,0:T(8,128)(2,1)S(1)} %copy-done.7, bf16[256,1792]{1,0:T(8,128)(2,1)S(1)} %copy-done.10, ...), custom_call_target="tpu_custom_call" | custom-call | flops 5637144576 | bytes 32509952 | tf_op jit(solution)/shard_map/weights_back/pallas_call | solution.py:72
  258.3 10.3 %collective-permute-done.57 = bf16[128,1792]{1,0:T(8,128)(2,1)S(1)} collective-permute-done((bf16[128,1792]{1,0:T(8,128)(2,1)S(1)}, bf16[128,1792]{1,0:T(8,128)(2,1)S(1)}, u32[]{:S(2)}, u32[]{:S(2)}) %collective-permute-start.57) | collective-permute-done | bytes 458784 | tf_op jit(solution)/shard_map/ppermute | solution.py:25
  277.1 10.8 %weights_back.5 = (bf16[7168,512]{1,0:T(8,128)(2,1)}, bf16[7168,512]{1,0:T(8,128)(2,1)}, bf16[512,7168]{1,0:T(8,128)(2,1)}) custom-call(s32[1]{0:T(128)} %bitcast.8._, bf16[256,1792]{1,0:T(8,128)(2,1)S(1)} %copy-done.4, bf16[256,1792]{1,0:T(8,128)(2,1)S(1)} %collective-permute-done.6.refs_1_, ...), custom_call_target="tpu_custom_call", output_to_operand_aliasing={{0}: (15, {}), {1}: (16, {}), {2}: (17, {})} | custom-call | flops 5637144576 | bytes 54530048 | tf_op jit(solution)/shard_map/weights_back/pallas_call | solution.py:72
  289.1 2.7 collective-permute-start.68
  293.3 11.1 %weights_back.6 = (bf16[7168,512]{1,0:T(8,128)(2,1)}, bf16[7168,512]{1,0:T(8,128)(2,1)}, bf16[512,7168]{1,0:T(8,128)(2,1)}) custom-call(s32[1]{0:T(128)} %bitcast.9._, bf16[256,1792]{1,0:T(8,128)(2,1)} %collective-permute-done.5.refs_0_, ...), custom_call_target="tpu_custom_call", output_to_operand_aliasing={{0}: (15, {}), {1}: (16, {}), {2}: (17, {})} | custom-call | flops 5637144576 | bytes 54530048 | tf_op jit(solution)/shard_map/weights_back/pallas_call | solution.py:72
  305.5 11.4 %weights_back.7 = (bf16[7168,512]{1,0:T(8,128)(2,1)}, bf16[7168,512]{1,0:T(8,128)(2,1)}, bf16[512,7168]{1,0:T(8,128)(2,1)}) custom-call(s32[1]{0:T(128)} %bitcast.1._, bf16[256,1792]{1,0:T(8,128)(2,1)} %collective-permute-done.14.refs_0_, ...), custom_call_target="tpu_custom_call", output_to_operand_aliasing={{0}: (15, {}), {1}: (16, {}), {2}: (17, {})} | custom-call | flops 5637144576 | bytes 54530048 | tf_op jit(solution)/shard_map/weights_back/pallas_call | solution.py:72
  (237 shorter events, 92.8 us)
Async XLA Ops:
  2.8 26.2 %collective-permute-start = (bf16[256,1792]{1,0:T(8,128)(2,1)S(1)}, bf16[256,1792]{1,0:T(8,128)(2,1)S(1)}, u32[]{:S(2)}, u32[]{:S(2)}) collective-permute-start(bf16[256,1792]{1,0:T(8,128)(2,1)S(1)} %constant_dynamic-update-slice_fusion.refs_0_), channel_id=1, source_target_pairs={{0,1},{1,2},{2,3},{3,0},{4,5},{5,6},{6,7},{7,4},{8,9},{9,10},{10,1... | collective-permute-start | bytes 2752520 | tf_op jit(solution)/shard_map/ppermute | solution.py:30
  5.9 23.1 %collective-permute-start.1 = (bf16[256,1792]{1,0:T(8,128)(2,1)S(1)}, bf16[256,1792]{1,0:T(8,128)(2,1)S(1)}, u32[]{:S(2)}, u32[]{:S(2)}) collective-permute-start(bf16[256,1792]{1,0:T(8,128)(2,1)S(1)} %constant_dynamic-update-slice_fusion.refs_0_), channel_id=1, source_target_pairs={{0,8},{4,12},{8,0},{12,4},{16,24},{20,28},{24,16},{28,20},{1,9},{5... | collective-permute-start | bytes 2752520 | tf_op jit(solution)/shard_map/ppermute | solution.py:25
  7.3 21.6 %collective-permute-start.2 = (bf16[256,1792]{1,0:T(8,128)(2,1)S(1)}, bf16[256,1792]{1,0:T(8,128)(2,1)S(1)}, u32[]{:S(2)}, u32[]{:S(2)}) collective-permute-start(bf16[256,1792]{1,0:T(8,128)(2,1)S(1)} %constant_dynamic-update-slice_fusion.refs_0_), channel_id=1, source_target_pairs={{0,16},{4,20},{8,24},{12,28},{16,0},{20,4},{24,8},{28,12},{1,17},{... | collective-permute-start | bytes 2752520 | tf_op jit(solution)/shard_map/ppermute | solution.py:25
  8.9 18.9 %collective-permute-start.3 = (f32[8,128]{1,0:T(8,128)S(1)}, f32[8,128]{1,0:T(8,128)S(1)}, u32[]{:S(2)}, u32[]{:S(2)}) collective-permute-start(f32[8,128]{1,0:T(8,128)S(1)} %bitcast.122), channel_id=1, source_target_pairs={{0,8},{4,12},{8,0},{12,4},{16,24},{20,28},{24,16},{28,20},{1,9},{5... | collective-permute-start | bytes 12296 | tf_op jit(solution)/shard_map/ppermute | solution.py:25
  9.5 19.5 %collective-permute-start.4 = (f32[8,128]{1,0:T(8,128)S(1)}, f32[8,128]{1,0:T(8,128)S(1)}, u32[]{:S(2)}, u32[]{:S(2)}) collective-permute-start(f32[8,128]{1,0:T(8,128)S(1)} %bitcast.123), channel_id=1, source_target_pairs={{0,16},{4,20},{8,24},{12,28},{16,0},{20,4},{24,8},{28,12},{1,17},{... | collective-permute-start | bytes 12296 | tf_op jit(solution)/shard_map/ppermute | solution.py:25
  29.0 22.7 %collective-permute-start.5 = (bf16[256,1792]{1,0:T(8,128)(2,1)S(1)}, bf16[256,1792]{1,0:T(8,128)(2,1)}, u32[]{:S(2)}, u32[]{:S(2)}) collective-permute-start(bf16[256,1792]{1,0:T(8,128)(2,1)S(1)} %collective-permute-done.refs_0_), channel_id=1, source_target_pairs={{0,1},{1,2},{2,3},{3,0},{4,5},{5,6},{6,7},{7,4},{8,9},{9,10},{10,1... | collective-permute-start | bytes 2752520 | tf_op jit(solution)/shard_map/ppermute | solution.py:30
  33.4 28.8 %collective-permute-start.6 = (bf16[256,1792]{1,0:T(8,128)(2,1)S(1)}, bf16[256,1792]{1,0:T(8,128)(2,1)S(1)}, u32[]{:S(2)}, u32[]{:S(2)}) collective-permute-start(bf16[256,1792]{1,0:T(8,128)(2,1)S(1)} %collective-permute-done.refs_0_), channel_id=1, source_target_pairs={{0,8},{4,12},{8,0},{12,4},{16,24},{20,28},{24,16},{28,20},{1,9},{5... | collective-permute-start | bytes 2752520 | tf_op jit(solution)/shard_map/ppermute | solution.py:25
  41.4 20.8 %collective-permute-start.7 = (bf16[256,1792]{1,0:T(8,128)(2,1)S(1)}, bf16[256,1792]{1,0:T(8,128)(2,1)S(1)}, u32[]{:S(2)}, u32[]{:S(2)}) collective-permute-start(bf16[256,1792]{1,0:T(8,128)(2,1)S(1)} %collective-permute-done.refs_0_), channel_id=1, source_target_pairs={{0,16},{4,20},{8,24},{12,28},{16,0},{20,4},{24,8},{28,12},{1,17},{... | collective-permute-start | bytes 2752520 | tf_op jit(solution)/shard_map/ppermute | solution.py:25
  42.9 19.3 %collective-permute-start.11 = (bf16[256,1792]{1,0:T(8,128)(2,1)S(1)}, bf16[256,1792]{1,0:T(8,128)(2,1)S(1)}, u32[]{:S(2)}, u32[]{:S(2)}) collective-permute-start(bf16[256,1792]{1,0:T(8,128)(2,1)S(1)} %constant_dynamic-update-slice_fusion.refs_0_), channel_id=1, source_target_pairs={{0,4},{4,0},{8,12},{12,8},{16,20},{20,16},{24,28},{28,24},{1,5},{5... | collective-permute-start | bytes 2752520 | tf_op jit(solution)/shard_map/ppermute | solution.py:25
  64.2 30.3 %collective-permute-start.15 = (bf16[256,1792]{1,0:T(8,128)(2,1)}, bf16[256,1792]{1,0:T(8,128)(2,1)S(1)}, u32[]{:S(2)}, u32[]{:S(2)}) collective-permute-start(bf16[256,1792]{1,0:T(8,128)(2,1)} %collective-permute-done.5.refs_0_), channel_id=1, source_target_pairs={{0,8},{4,12},{8,0},{12,4},{16,24},{20,28},{24,16},{28,20},{1,9},{5... | collective-permute-start | bytes 2752520 | tf_op jit(solution)/shard_map/ppermute | solution.py:25
  68.3 25.1 %collective-permute-start.22 = (bf16[128,1792]{1,0:T(8,128)(2,1)}, bf16[128,1792]{1,0:T(8,128)(2,1)}, u32[]{:S(2)}, u32[]{:S(2)}) collective-permute-start(bf16[128,1792]{1,0:T(8,128)(2,1)} %slice.151), channel_id=1, source_target_pairs={{0,8},{4,12},{8,0},{12,4},{16,24},{20,28},{24,16},{28,20},{1,9},{5... | collective-permute-start | bytes 1376264 | tf_op jit(solution)/shard_map/ppermute | solution.py:25
  69.4 24.5 %collective-permute-start.26 = (bf16[128,1792]{1,0:T(8,128)(2,1)}, bf16[128,1792]{1,0:T(8,128)(2,1)}, u32[]{:S(2)}, u32[]{:S(2)}) collective-permute-start(bf16[128,1792]{1,0:T(8,128)(2,1)} %collective-permute-done.9.refs_3_), channel_id=1, source_target_pairs={{0,4},{4,0},{8,12},{12,8},{16,20},{20,16},{24,28},{28,24},{1,5},{5... | collective-permute-start | bytes 1376264 | tf_op jit(solution)/shard_map/ppermute | solution.py:25
  69.4 24.5 %collective-permute-start.27 = (bf16[128,1792]{1,0:T(8,128)(2,1)}, bf16[128,1792]{1,0:T(8,128)(2,1)}, u32[]{:S(2)}, u32[]{:S(2)}) collective-permute-start(bf16[128,1792]{1,0:T(8,128)(2,1)} %collective-permute-done.10.refs_4_), channel_id=1, source_target_pairs={{0,4},{4,0},{8,12},{12,8},{16,20},{20,16},{24,28},{28,24},{1,5},{5... | collective-permute-start | bytes 1376264 | tf_op jit(solution)/shard_map/ppermute | solution.py:25
  80.5 31.5 %collective-permute-start.14 = (bf16[256,1792]{1,0:T(8,128)(2,1)}, bf16[256,1792]{1,0:T(8,128)(2,1)}, u32[]{:S(2)}, u32[]{:S(2)}) collective-permute-start(bf16[256,1792]{1,0:T(8,128)(2,1)} %collective-permute-done.5.refs_0_), channel_id=1, source_target_pairs={{0,1},{1,2},{2,3},{3,0},{4,5},{5,6},{6,7},{7,4},{8,9},{9,10},{10,1... | collective-permute-start | bytes 2752520 | tf_op jit(solution)/shard_map/ppermute | solution.py:30
  115.9 32.7 %collective-permute-start.28 = (bf16[256,1792]{1,0:T(8,128)(2,1)}, bf16[256,1792]{1,0:T(8,128)(2,1)}, u32[]{:S(2)}, u32[]{:S(2)}) collective-permute-start(bf16[256,1792]{1,0:T(8,128)(2,1)} %collective-permute-done.14.refs_0_), channel_id=1, source_target_pairs={{0,8},{4,12},{8,0},{12,4},{16,24},{20,28},{24,16},{28,20},{1,9},{5... | collective-permute-start | bytes 2752520 | tf_op jit(solution)/shard_map/ppermute | solution.py:25
  125.1 23.5 %collective-permute-start.29 = (bf16[256,1792]{1,0:T(8,128)(2,1)}, bf16[256,1792]{1,0:T(8,128)(2,1)}, u32[]{:S(2)}, u32[]{:S(2)}) collective-permute-start(bf16[256,1792]{1,0:T(8,128)(2,1)} %collective-permute-done.14.refs_0_), channel_id=1, source_target_pairs={{0,16},{4,20},{8,24},{12,28},{16,0},{20,4},{24,8},{28,12},{1,17},{... | collective-permute-start | bytes 2752520 | tf_op jit(solution)/shard_map/ppermute | solution.py:25
  128.2 20.4 %collective-permute-start.32 = (bf16[256,1792]{1,0:T(8,128)(2,1)}, bf16[256,1792]{1,0:T(8,128)(2,1)}, u32[]{:S(2)}, u32[]{:S(2)}) collective-permute-start(bf16[256,1792]{1,0:T(8,128)(2,1)} %collective-permute-done.5.refs_0_), channel_id=1, source_target_pairs={{0,4},{4,0},{8,12},{12,8},{16,20},{20,16},{24,28},{28,24},{1,5},{5... | collective-permute-start | bytes 2752520 | tf_op jit(solution)/shard_map/ppermute | solution.py:25
  129.0 19.6 %collective-permute-start.33 = (bf16[256,1792]{1,0:T(8,128)(2,1)S(1)}, bf16[256,1792]{1,0:T(8,128)(2,1)}, u32[]{:S(2)}, u32[]{:S(2)}) collective-permute-start(bf16[256,1792]{1,0:T(8,128)(2,1)S(1)} %collective-permute-done.15.refs_1_), channel_id=1, source_target_pairs={{0,4},{4,0},{8,12},{12,8},{16,20},{20,16},{24,28},{28,24},{1,5},{5... | collective-permute-start | bytes 2752520 | tf_op jit(solution)/shard_map/ppermute | solution.py:25
  149.3 18.8 %collective-permute-start.39 = (bf16[256,1792]{1,0:T(8,128)(2,1)}, bf16[256,1792]{1,0:T(8,128)(2,1)}, u32[]{:S(2)}, u32[]{:S(2)}) collective-permute-start(bf16[256,1792]{1,0:T(8,128)(2,1)} %collective-permute-done.14.refs_0_), channel_id=1, source_target_pairs={{0,4},{4,0},{8,12},{12,8},{16,20},{20,16},{24,28},{28,24},{1,5},{5... | collective-permute-start | bytes 2752520 | tf_op jit(solution)/shard_map/ppermute | solution.py:25
  218.5 19.1 %collective-permute-start.54 = (bf16[512,1792]{1,0:T(8,128)(2,1)S(1)}, bf16[512,1792]{1,0:T(8,128)(2,1)}, u32[]{:S(2)}, u32[]{:S(2)}) collective-permute-start(bf16[512,1792]{1,0:T(8,128)(2,1)S(1)} %get-tuple-element.172), channel_id=1, source_target_pairs={{0,4},{4,0},{8,12},{12,8},{16,20},{20,16},{24,28},{28,24},{1,5},{5... | collective-permute-start | bytes 5505032 | tf_op jit(solution)/shard_map/ppermute | solution.py:25
  237.6 20.7 %collective-permute-start.56 = (bf16[128,1792]{1,0:T(8,128)(2,1)S(1)}, bf16[128,1792]{1,0:T(8,128)(2,1)S(1)}, u32[]{:S(2)}, u32[]{:S(2)}) collective-permute-start(bf16[128,1792]{1,0:T(8,128)(2,1)S(1)} %add_convert_fusion.7), channel_id=1, source_target_pairs={{0,1},{1,2},{2,3},{3,0},{4,5},{5,6},{6,7},{7,4},{8,9},{9,10},{10,1... | collective-permute-start | bytes 1376264 | tf_op jit(solution)/shard_map/ppermute | solution.py:30
  239.2 19.1 %collective-permute-start.58 = (bf16[128,1792]{1,0:T(8,128)(2,1)S(1)}, bf16[128,1792]{1,0:T(8,128)(2,1)}, u32[]{:S(2)}, u32[]{:S(2)}) collective-permute-start(bf16[128,1792]{1,0:T(8,128)(2,1)S(1)} %get-tuple-element.176), channel_id=1, source_target_pairs={{0,16},{4,20},{8,24},{12,28},{16,0},{20,4},{24,8},{28,12},{1,17},{... | collective-permute-start | bytes 1376264 | tf_op jit(solution)/shard_map/ppermute | solution.py:25
  244.8 25.2 %collective-permute-start.55 = (bf16[512,1792]{1,0:T(8,128)(2,1)S(1)}, bf16[512,1792]{1,0:T(8,128)(2,1)}, u32[]{:S(2)}, u32[]{:S(2)}) collective-permute-start(bf16[512,1792]{1,0:T(8,128)(2,1)S(1)} %get-tuple-element.173), channel_id=1, source_target_pairs={{0,4},{4,0},{8,12},{12,8},{16,20},{20,16},{24,28},{28,24},{1,5},{5... | collective-permute-start | bytes 5505032 | tf_op jit(solution)/shard_map/ppermute | solution.py:25
  270.0 18.9 %collective-permute-start.62 = (bf16[128,1792]{1,0:T(8,128)(2,1)S(1)}, bf16[128,1792]{1,0:T(8,128)(2,1)S(1)}, u32[]{:S(2)}, u32[]{:S(2)}) collective-permute-start(bf16[128,1792]{1,0:T(8,128)(2,1)S(1)} %add_convert_fusion.6), channel_id=1, source_target_pairs={{0,1},{1,2},{2,3},{3,0},{4,5},{5,6},{6,7},{7,4},{8,9},{9,10},{10,1... | collective-permute-start | bytes 1376264 | tf_op jit(solution)/shard_map/ppermute | solution.py:30
  (79 other events, 827.5 us)
